TPU v7x, 256 devices: a whole 4x4x8 slice. The times are simulated.
256 devices in a mesh: group: 32 (over y, z_hi, core), tensor: 4 (over x), dp: 2 (over z_lo).
Axes of the slice: x: 4, y: 4, z: 8 (z_hi: 4, z_lo: 2; z = z_hi * 2 + z_lo), core: 2. Of those that a mesh axis runs over, the one named last changes fastest.
Arguments:
- queries: bfloat16 [2, 32, 256, 5120], P('dp', 'group', 'tensor'), may hold values from -32 to 32
- suffix_keys: bfloat16 [2, 32, 256, 1024], P('dp', 'group', 'tensor'), may hold values from -6 to 6
- suffix_values: bfloat16 [2, 32, 256, 1024], P('dp', 'group', 'tensor'), may hold values from -6 to 6
- d_out: bfloat16 [2, 32, 256, 5120], P('dp', 'group', 'tensor'), may hold values from -6 to 6
- prefix_keys: bfloat16 [2, 1024, 1024], P('dp', 'group', 'tensor'), may hold values from -12 to 12
- prefix_values: bfloat16 [2, 1024, 1024], P('dp', 'group', 'tensor'), may hold values from -6 to 6
- advantages: float32 [2, 32], P('dp', 'group'), may hold values from -4 to 4
- lengths: int32 [2, 32], P('dp', 'group'), may hold values from 64 to 256, as said below
Outputs:
- grad_queries: bfloat16 [2, 32, 256, 5120], P('dp', 'group', None, 'tensor')
- grad_suffix_keys: bfloat16 [2, 32, 256, 1024], P('dp', 'group', None, 'tensor')
- grad_suffix_values: bfloat16 [2, 32, 256, 1024], P('dp', 'group', None, 'tensor')
- grad_prefix_keys: bfloat16 [2, 1024, 1024], P('dp', 'group', 'tensor')
- grad_prefix_values: bfloat16 [2, 1024, 1024], P('dp', 'group', 'tensor')
- grad_query_bias: float32 [5120], P('tensor')
- grad_kv_bias: float32 [2, 1024], P(None, 'tensor')
Inputs may be any that keep to these rules, and one draw needn't show every extreme that they name: `lengths`: in every prompt some rollout has length 256.
All inputs are finite; a program needn't handle non-finite values.
Results may differ from a plain program's by a relative error of at most 0.02.
Values may be sent and summed in bfloat16 or wider, within the bound.
A program may use at most 64 MiB of HBM per device.

v0:
```python
import jax
import jax.numpy as jnp
from jax import lax
from jax.sharding import PartitionSpec as P

H = 40
KEY_VALUE_HEADS = 8
HEAD_SIZE = 128


block_rows = 512


def local(
    queries, suffix_keys, suffix_values, d_out, prefix_keys, prefix_values, advantages, lengths
):
    moved = (
        lax.all_to_all(queries, "tensor", split_axis=3, concat_axis=2, tiled=True),
        lax.all_to_all(d_out, "tensor", split_axis=3, concat_axis=2, tiled=True),
        lax.all_to_all(suffix_keys, "tensor", split_axis=3, concat_axis=2, tiled=True),
        lax.all_to_all(suffix_values, "tensor", split_axis=3, concat_axis=2, tiled=True),
    )
    q_all, cot_raw, key_suf, val_suf = moved
    rollouts = q_all.shape[1]
    resp = q_all.shape[2]
    kv_local = key_suf.shape[3] // HEAD_SIZE
    ratio = H // KEY_VALUE_HEADS
    scale = HEAD_SIZE ** (-0.5)
    cols = kv_local * HEAD_SIZE
    q5 = q_all[0].reshape(rollouts, resp, kv_local, ratio, HEAD_SIZE)
    keys4 = key_suf[0].reshape(rollouts, resp, kv_local, HEAD_SIZE)
    vals4 = val_suf[0].reshape(rollouts, resp, kv_local, HEAD_SIZE)
    lens = lengths[0]
    weight = advantages[0] / lens.astype(jnp.float32)
    positions = jnp.arange(resp, dtype=jnp.int32)
    valid = positions[None, :] < lens[:, None]
    factor = weight[:, None] * valid.astype(jnp.float32)
    cot5 = (cot_raw[0].astype(jnp.float32) * factor[:, :, None]).astype(jnp.bfloat16)
    cot5 = cot5.reshape(rollouts, resp, kv_local, ratio, HEAD_SIZE)
    allowed = (positions[None, :] <= positions[:, None])[None] & (
        positions[None, None, :] < lens[:, None, None]
    )
    seen = allowed[:, None, None]
    suf_scores = (
        jnp.einsum("rtkgd,rskd->rkgts", q5, keys4, preferred_element_type=jnp.float32) * scale
    )
    suf_scores = jnp.where(seen, suf_scores, -jnp.inf)
    suf_dprobs = jnp.einsum("rtkgd,rskd->rkgts", cot5, vals4, preferred_element_type=jnp.float32)
    top0 = jnp.max(suf_scores, axis=-1)
    expd0 = jnp.exp(suf_scores - top0[..., None])
    carry = (top0, jnp.sum(expd0, axis=-1), jnp.sum(expd0 * suf_dprobs, axis=-1))
    whole_keys, whole_vals = (
        lax.all_gather(prefix_keys[0], "group", axis=0, tiled=True),
        lax.all_gather(prefix_values[0], "group", axis=0, tiled=True),
    )
    prefix_total = whole_keys.shape[0]
    for begin in range(0, prefix_total, block_rows):
        kblock = whole_keys[begin : begin + block_rows].reshape(-1, kv_local, HEAD_SIZE)
        vblock = whole_vals[begin : begin + block_rows].reshape(-1, kv_local, HEAD_SIZE)
        scores = (
            jnp.einsum("rtkgd,pkd->rkgtp", q5, kblock, preferred_element_type=jnp.float32) * scale
        )
        dprobs = jnp.einsum("rtkgd,pkd->rkgtp", cot5, vblock, preferred_element_type=jnp.float32)
        top, total, accum = carry
        newtop = jnp.maximum(top, jnp.max(scores, axis=-1))
        shrink = jnp.exp(top - newtop)
        expd = jnp.exp(scores - newtop[..., None])
        carry = (
            newtop,
            total * shrink + jnp.sum(expd, axis=-1),
            accum * shrink + jnp.sum(expd * dprobs, axis=-1),
        )
    top, total, accum = carry
    delta = accum / total
    query_gradient = jnp.zeros(q5.shape, jnp.float32)
    pieces = []
    for begin in range(0, prefix_total, block_rows):
        kblock = whole_keys[begin : begin + block_rows].reshape(-1, kv_local, HEAD_SIZE)
        vblock = whole_vals[begin : begin + block_rows].reshape(-1, kv_local, HEAD_SIZE)
        block_scores = (
            jnp.einsum("rtkgd,pkd->rkgtp", q5, kblock, preferred_element_type=jnp.float32) * scale
        )
        probs = jnp.exp(block_scores - top[..., None]) / total[..., None]
        block_probs_b = probs.astype(jnp.bfloat16)
        block_dprobs = jnp.einsum(
            "rtkgd,pkd->rkgtp", cot5, vblock, preferred_element_type=jnp.float32
        )
        block_dscores = (probs * (block_dprobs - delta[..., None])).astype(jnp.bfloat16)
        query_gradient = query_gradient + scale * jnp.einsum(
            "rkgtp,pkd->rtkgd", block_dscores, kblock, preferred_element_type=jnp.float32
        )
        rows_here = kblock.shape[0]
        key_gradient = scale * jnp.einsum(
            "rkgtp,rtkgd->pkd", block_dscores, q5, preferred_element_type=jnp.float32
        )
        value_gradient = jnp.einsum(
            "rkgtp,rtkgd->pkd", block_probs_b, cot5, preferred_element_type=jnp.float32
        )
        pieces.append(
            jnp.concatenate(
                [key_gradient.reshape(rows_here, -1), value_gradient.reshape(rows_here, -1)], axis=1
            )
        )
    buffer = jnp.concatenate(pieces, axis=0)
    summed = lax.psum_scatter(
        buffer.astype(jnp.bfloat16), "group", scatter_dimension=0, tiled=True
    ).astype(jnp.float32)
    probs_s = jnp.exp(suf_scores - top[..., None]) / total[..., None]
    probs_sb = probs_s.astype(jnp.bfloat16)
    dscores_s = (probs_s * (suf_dprobs - delta[..., None])).astype(jnp.bfloat16)
    query_gradient = query_gradient + scale * jnp.einsum(
        "rkgts,rskd->rtkgd", dscores_s, keys4, preferred_element_type=jnp.float32
    )
    dkey_suf = scale * jnp.einsum(
        "rkgts,rtkgd->rskd", dscores_s, q5, preferred_element_type=jnp.float32
    )
    dval_suf = jnp.einsum("rkgts,rtkgd->rskd", probs_sb, cot5, preferred_element_type=jnp.float32)
    query_bias = jnp.sum(query_gradient, axis=(0, 1)).reshape(-1)
    kv_bias = jnp.stack(
        [jnp.sum(dkey_suf, axis=(0, 1)).reshape(-1), jnp.sum(dval_suf, axis=(0, 1)).reshape(-1)]
    )
    query_bias, kv_bias = lax.psum((query_bias, kv_bias), ("group", "dp"))
    grad_queries = query_gradient.reshape(rollouts, resp, -1).astype(jnp.bfloat16)[None]
    grad_suffix_keys = dkey_suf.reshape(rollouts, resp, cols).astype(jnp.bfloat16)[None]
    grad_suffix_values = dval_suf.reshape(rollouts, resp, cols).astype(jnp.bfloat16)[None]
    grad_prefix_keys = summed[:, :cols].astype(jnp.bfloat16)[None]
    grad_prefix_values = summed[:, cols:].astype(jnp.bfloat16)[None]
    return (
        grad_queries,
        grad_suffix_keys,
        grad_suffix_values,
        grad_prefix_keys,
        grad_prefix_values,
        query_bias,
        kv_bias,
    )


def solution(mesh):
    in_specs = (
        P("dp", "group", "tensor", None),
        P("dp", "group", "tensor", None),
        P("dp", "group", "tensor", None),
        P("dp", "group", "tensor", None),
        P("dp", "group", "tensor"),
        P("dp", "group", "tensor"),
        P("dp", "group"),
        P("dp", "group"),
    )
    out_specs = (
        P("dp", "group", None, "tensor"),
        P("dp", "group", None, "tensor"),
        P("dp", "group", None, "tensor"),
        P("dp", "group", "tensor"),
        P("dp", "group", "tensor"),
        P("tensor"),
        P(None, "tensor"),
    )
    return jax.shard_map(local, mesh=mesh, in_specs=in_specs, out_specs=out_specs, check_vma=False)
```

profile of v0, /device:TPU:4, one launch (start us, length us, event | category | flops | bytes accessed | tf_op | source)
XLA Modules:
  0.0 534.7 jit_solution(1142401842825056395)
XLA Ops:
  7.2 1.2 copy.193
  8.9 2.3 reduce.10
  12.1 5.5 %all-to-all-start.1 = ((bf16[4,2,8192]{2,1,0:T(2,128)(2,1)}), bf16[4,2,8192]{2,1,0:T(2,128)(2,1)S(1)}, u32[]{:S(2)}, u32[]{:S(2)}) async-start(bf16[4,2,8192]{2,1,0:T(2,128)(2,1)} %reshape.454), calls=%async_computation.1 | async-start | bytes 262144 | tf_op jit(solution)/shard_map/all_to_all | solution.py:20
  17.7 48.7 %all-gather = bf16[1,1024,256]{2,1,0:T(8,128)(2,1)S(1)} all-gather(bf16[1,32,256]{2,1,0:T(8,128)(2,1)} %param.12), channel_id=2, replica_groups=mesh['group'=32,'tensor'=4,'dp'=2] {'group'}, dimensions={1}, use_global_device_ids=true | all-gather | bytes 540672 | tf_op jit(solution)/shard_map/all_gather | solution.py:53
  66.4 43.7 %all-gather.1 = bf16[1,1024,256]{2,1,0:T(8,128)(2,1)} all-gather(bf16[1,32,256]{2,1,0:T(8,128)(2,1)S(1)} %copy-done.22), channel_id=3, replica_groups=mesh['group'=32,'tensor'=4,'dp'=2] {'group'}, dimensions={1}, use_global_device_ids=true | all-gather | bytes 540672 | tf_op jit(solution)/shard_map/all_gather | solution.py:54
  110.5 2.3 reduce.12
  113.7 4.8 all-to-all-start.3
  119.2 1.9 copy.188
  121.1 28.9 %reduce.9 = bf16[5120,64]{1,0:T(8,128)(2,1)} reduce(bf16[5120,1,1,64]{3,2,1,0:T(2,128)(2,1)S(1)} %bitcast.295, bf16[]{:T(256)} %broadcast.150), dimensions={1,2}, to_apply=%bitcast.251.reduce_sub_computation | reduce | bytes 1310722
  150.0 2.9 reshape.452
  152.9 5.3 all-to-all-start
  161.3 4.7 copy.201
  166.0 28.9 %reduce.11 = bf16[5120,64]{1,0:T(8,128)(2,1)} reduce(bf16[5120,1,1,64]{3,2,1,0:T(2,128)(2,1)S(1)} %bitcast.292, bf16[]{:T(256)} %broadcast.150), dimensions={1,2}, to_apply=%bitcast.249.reduce_sub_computation | reduce | bytes 1310722
  194.9 2.8 reshape.450
  197.8 1.8 copy.283
  202.8 1.2 reshape.457
  205.1 4.8 all-to-all-start.2
  211.1 1.5 copy.189
  213.1 1.7 copy.284
  215.7 3.8 bitcast_reduce_fusion
  219.5 3.8 bitcast_reduce_fusion.1
  223.3 2.6 reshape.451
  225.9 4.0 bitcast_convert_fusion
  229.9 2.1 copy.202
  232.1 1.7 reshape.422
  233.7 1.6 fusion.70
  235.4 2.1 fusion.36
  238.7 1.6 fusion.12
  240.9 1.6 fusion.10
  242.5 2.0 fusion.49
  244.5 2.0 fusion.46
  246.5 1.7 fusion.33
  248.2 3.9 fusion.14
  252.1 1.5 copy-done.1
  253.6 1.7 fusion.53
  255.3 1.8 copy.226
  257.1 1.8 copy.227
  258.9 3.4 fusion.52
  262.3 1.8 copy.232
  264.1 1.8 copy.233
  265.8 2.2 maximum_maximum_fusion
  268.1 2.4 fusion.71
  272.0 1.2 fusion.65
  273.2 1.9 fusion.69
  275.8 2.0 fusion.68
  278.5 1.1 copy.234
  279.6 246.7 %all-reduce = (f32[1280]{0:T(1024)}, f32[2,256]{1,0:T(2,128)}) all-reduce(f32[1280]{0:T(1024)S(1)} %reshape.421, f32[2,256]{1,0:T(2,128)S(1)} %pad_maximum_fusion), channel_id=1, replica_groups=mesh['group'=32,'tensor'=4,'dp'=2] {'group','dp'}, use_global_device_ids=true, to_apply=%region_11.12 | all-reduce | flops 1792 | bytes 14336 | tf_op jit(solution)/shard_map/psum | solution.py:122
  526.3 1.3 slice_bitcast_fusion
  (95 shorter events, 16.7 us)
Async XLA Ops:
  7.2 59.2 %copy-start.22 = (bf16[1,32,256]{2,1,0:T(8,128)(2,1)S(1)}, bf16[1,32,256]{2,1,0:T(8,128)(2,1)}, u32[]{:S(2)}) copy-start(bf16[1,32,256]{2,1,0:T(8,128)(2,1)} %param.13) | copy-start | bytes 49156
  7.2 102.9 %copy-start.19 = (bf16[1,1,64,1024]{3,2,1,0:T(8,128)(2,1)S(1)}, bf16[1,1,64,1024]{3,2,1,0:T(8,128)(2,1)}, u32[]{:S(2)}) copy-start(bf16[1,1,64,1024]{3,2,1,0:T(8,128)(2,1)} %param.10) | copy-start | bytes 393220
  11.2 108.0 %copy-start.13 = (bf16[1,1,64,5120]{3,2,1,0:T(8,128)(2,1)S(1)}, bf16[1,1,64,5120]{3,2,1,0:T(8,128)(2,1)}, u32[]{:S(2)}) copy-start(bf16[1,1,64,5120]{3,2,1,0:T(8,128)(2,1)} %param.8) | copy-start | bytes 1966084
  12.1 101.5 %all-to-all-start.1 = ((bf16[4,2,8192]{2,1,0:T(2,128)(2,1)}), bf16[4,2,8192]{2,1,0:T(2,128)(2,1)S(1)}, u32[]{:S(2)}, u32[]{:S(2)}) async-start(bf16[4,2,8192]{2,1,0:T(2,128)(2,1)} %reshape.454), calls=%async_computation.1 | async-start | bytes 262144 | tf_op jit(solution)/shard_map/all_to_all | solution.py:20
  113.7 4.8 copy-start.14
  113.7 39.2 %all-to-all-start.3 = ((bf16[4,2,8192]{2,1,0:T(2,128)(2,1)}), bf16[4,2,8192]{2,1,0:T(2,128)(2,1)}, u32[]{:S(2)}, u32[]{:S(2)}) async-start(bf16[4,2,8192]{2,1,0:T(2,128)(2,1)} %reshape.456), calls=%async_computation.3 | async-start | bytes 262144 | tf_op jit(solution)/shard_map/all_to_all | solution.py:21
  150.0 8.1 %copy-start.7 = (bf16[1,1024,256]{2,1,0:T(8,128)(2,1)S(1)}, bf16[1,1024,256]{2,1,0:T(8,128)(2,1)}, u32[]{:S(2)}) copy-start(bf16[1,1024,256]{2,1,0:T(8,128)(2,1)} %all-gather.1) | copy-start | bytes 1572868
  150.0 10.5 %copy-start.11 = (bf16[1,512,256]{2,1,0:T(8,128)(2,1)S(1)}, bf16[1,512,256]{2,1,0:T(8,128)(2,1)}, u32[]{:S(2)}) copy-start(bf16[1,512,256]{2,1,0:T(8,128)(2,1)} %get-tuple-element.57) | copy-start | bytes 786436
  152.9 52.2 %all-to-all-start = ((bf16[4,2,40960]{2,1,0:T(2,128)(2,1)}), bf16[4,2,40960]{2,1,0:T(2,128)(2,1)S(1)}, u32[]{:S(2)}, u32[]{:S(2)}) async-start(bf16[4,2,40960]{2,1,0:T(2,128)(2,1)} %reshape.452), calls=%async_computation | async-start | bytes 1310720 | tf_op jit(solution)/shard_map/all_to_all | solution.py:18
  194.9 4.7 copy-start.12
  194.9 6.3 %copy-start.15 = (bf16[4,2,8192]{2,1,0:T(2,128)(2,1)S(1)}, bf16[4,2,8192]{2,1,0:T(2,128)(2,1)}, u32[]{:S(2)}) copy-start(bf16[4,2,8192]{2,1,0:T(2,128)(2,1)} %copy-done.14) | copy-start | bytes 393220
  205.1 18.1 %all-to-all-start.2 = ((bf16[4,2,40960]{2,1,0:T(2,128)(2,1)}), bf16[4,2,40960]{2,1,0:T(2,128)(2,1)}, u32[]{:S(2)}, u32[]{:S(2)}) async-start(bf16[4,2,40960]{2,1,0:T(2,128)(2,1)} %reshape.450), calls=%async_computation.2 | async-start | bytes 1310720 | tf_op jit(solution)/shard_map/all_to_all | solution.py:19
  209.9 316.4 %reduce-scatter.2.cloned.1.call-start = ((), (), s32[]{:S(2)}) async-start(), calls=%async_computation.5 | async-start | bytes 1081344 | tf_op jit(solution)/shard_map/reduce_scatter | solution.py:105
  212.6 3.0 copy-start.5
  233.7 3.8 copy-start.20
  233.7 3.8 copy-start.21
  233.7 3.8 copy-start.16
  233.7 4.5 slice-start
  235.4 2.9 slice-start.1
  237.5 7.0 %copy-start.3 = (bf16[256,2,5,128]{3,0,2,1:T(8,128)(2,1)}, bf16[256,2,5,128]{3,0,2,1:T(8,128)(2,1)S(1)}, u32[]{:S(2)}) copy-start(bf16[256,2,5,128]{3,0,2,1:T(8,128)(2,1)S(1)} %fusion.36) | copy-start | bytes 1966084
  237.6 1.2 copy-start.10
  238.2 2.2 slice-start.2
  238.7 2.1 slice-start.3
  238.7 2.1 copy-start.9
  242.5 5.7 %copy-start.17 = (f32[2,5,256]{2,1,0:T(8,128)}, f32[2,5,256]{2,1,0:T(8,128)S(1)}, u32[]{:S(2)}) copy-start(f32[2,5,256]{2,1,0:T(8,128)S(1)} %get-tuple-element.62) | copy-start | bytes 30724
  252.1 1.5 copy-start.1
  268.1 2.5 copy-start
  268.1 2.5 copy-start.6
  270.6 1.3 copy-start.2
  270.6 1.3 copy-start.8
  272.0 1.2 copy-start.18
  275.0 3.5 copy-start.4
Sparse Core Ops, SparseCore 0:
  268.2 84.7 reduce-scatter.1
where the time goes:
time: 544 us; the launch traced here: 535 us
  blocking collectives  339 us (62%)
  other arithmetic  77.2 us (14%)
  local copies, waits for them, and re-layouts  51.7 us (10%)
  matrix products  30.1 us (6%)
  starting transfers between devices  20.6 us (4%)
  between operations  16.1 us (3%)
    psum x1, blocking collectives, local(): query_bias, kv_bias = lax.psum((query_bias, kv_bias), ('group', 'dp'))  247 us
    unnamed x6, other arithmetic  62.4 us
    all_gather x1, blocking collectives, local(): lax.all_gather(prefix_keys[0], 'group', axis=0, tiled=True)  48.7 us
    all_gather x1, blocking collectives, local(): lax.all_gather(prefix_values[0], 'group', axis=0, tiled=True)  43.7 us
    unnamed x74, local copies, waits for them, and re-layouts  31.1 us
  transfers between devices with their start and end apart: 5, of which 0 were waited for; matrix products, arithmetic and copies ran while one was open for 20% of the time, Pallas kernels for 0%

commit v1 on v0

v1 whole, which is shorter than its diff:
```python
import math

import jax
import jax.numpy as jnp
from jax import lax
from jax.experimental import pallas as pl
from jax.experimental.pallas import tpu as pltpu
from jax.sharding import PartitionSpec as P

H = 40
KEY_VALUE_HEADS = 8
D = 128
RATIO = H // KEY_VALUE_HEADS
NX = 4
NY = 4
NZ = 4
KV = KEY_VALUE_HEADS // NX
TOK = 64
RESP = NX * TOK
QC = RATIO * D
PRE = 1024
KEYS = PRE + RESP
PIECE = PRE // (2 * NY * NZ)
YROWS = NZ * PIECE
HALF = NY * YROWS
QT = RATIO * RESP
SCALE = D ** -0.5
C2 = SCALE * math.log2(math.e)
MESH = pl.DeviceIdType.MESH
F32 = jnp.float32
BF16 = jnp.bfloat16


def nt(a, b):
    return lax.dot_general(a, b, (((1,), (1,)), ((), ())), preferred_element_type=F32)


def nn(a, b):
    return lax.dot_general(a, b, (((1,), (0,)), ((), ())), preferred_element_type=F32)


def fold(a, op):
    return op(a.reshape(a.shape[0] // 8, 8, a.shape[1]), axis=0)


def kernel(
    q_in, ks_in, vs_in, do_in, pk_in, pv_in, adv_ref, len_ref,
    dq_out, dks_out, dvs_out, dpk_out, dpv_out, qb_out, kvb_out,
    q_all, do_all, k_all, v_all, k_t, q_st, c_st, s_buf, dp_buf, p_all, ds_all,
    dq_v, dks_v, dvs_v, rs_snd, rs_sib, rs_own, rs_ysnd, rs_y, rs_zsum, rs_zsnd, rs_z, dpk_v, dpv_v,
    b_own, b_sib, b_y, b_z, qb_v, kvb_v,
    xs, xr, xl, gzs, gzr, gzl, gys, gyr, gss, gsr,
    r0s, r0r, r1s, r1r, r2s, r2r, bs0, br0, bs1, br1, bs2, br2, osem,
):
    g = lax.axis_index("group")
    x = lax.axis_index("tensor")
    dp = lax.axis_index("dp")
    core = lax.rem(g, 2)
    zh = lax.rem(g // 2, NZ)
    y = g // (2 * NZ)
    sib = {"group": g + 1 - 2 * core}

    def xdev(d):
        return {"tensor": lax.rem(x + d, NX)}

    def ydev(d):
        return {"group": lax.rem(y + d, NY) * (2 * NZ) + zh * 2 + core}

    def zdev(d):
        return {"group": y * (2 * NZ) + lax.rem(zh + d, NZ) * 2 + core}

    zpos = zh * 2 + dp

    def zzdev(d):
        p = lax.rem(zpos + d, 2 * NZ)
        return {"group": y * (2 * NZ) + (p // 2) * 2 + core, "dp": lax.rem(p, 2)}

    def remote(src, dst, ss, rs, dev):
        return pltpu.make_async_remote_copy(
            src_ref=src, dst_ref=dst, send_sem=ss, recv_sem=rs, device_id=dev, device_id_type=MESH
        )

    barrier = pltpu.get_barrier_semaphore()
    peers = [sib] + [xdev(d) for d in range(1, NX)] + [ydev(d) for d in range(1, NY)]
    peers += [zzdev(d) for d in range(1, 2 * NZ)]
    for dev in peers:
        pl.semaphore_signal(barrier, inc=1, device_id=dev, device_id_type=MESH)

    def cols(owner, kv):
        return pl.ds(pl.multiple_of(owner * (KV * QC) + kv * QC, D), QC)

    def kcols(owner):
        return pl.ds(pl.multiple_of(owner * (KV * D), D), KV * D)

    def trow(owner, base=0):
        return pl.ds(pl.multiple_of(base + owner * TOK, TOK), TOK)

    def xsrc(kind, owner):
        if kind in (0, 4):
            return q_in.at[:, cols(owner, kind // 4)]
        if kind in (1, 5):
            return do_in.at[:, cols(owner, kind // 4)]
        return (ks_in if kind == 2 else vs_in).at[:, kcols(owner)]

    def xdst(kind, source):
        if kind in (0, 4):
            return q_all.at[kind // 4, trow(source)]
        if kind in (1, 5):
            return do_all.at[kind // 4, trow(source)]
        return (k_all if kind == 2 else v_all).at[trow(source, PRE)]

    def xsend(kind, d):
        return remote(
            xsrc(kind, lax.rem(x + d, NX)), xdst(kind, x), xs.at[kind, d - 1], xr.at[kind, d - 1], xdev(d)
        )

    def xrecv(kind, d):
        dst = xdst(kind, lax.rem(x + NX - d, NX))
        return remote(dst, dst, xs.at[kind, d - 1], xr.at[kind, d - 1], xdev(d))

    def xlocal(kind):
        return pltpu.make_async_copy(xsrc(kind, x), xdst(kind, x), xl.at[kind])

    def prow(c, yy, zz, n=PIECE):
        return pl.ds(pl.multiple_of(c * HALF + yy * YROWS + zz * PIECE, PIECE), n)

    full = (k_all, v_all)
    piece = (pk_in, pv_in)

    def gz(kind, d):
        return remote(piece[kind], full[kind].at[prow(core, y, zh)], gzs.at[kind, d - 1], gzr.at[kind, d - 1], zdev(d))

    def gz_recv(kind, d):
        dst = full[kind].at[prow(core, y, lax.rem(zh + NZ - d, NZ))]
        return remote(dst, dst, gzs.at[kind, d - 1], gzr.at[kind, d - 1], zdev(d))

    def gz_local(kind):
        return pltpu.make_async_copy(piece[kind], full[kind].at[prow(core, y, zh)], gzl.at[kind])

    def gy(kind, d):
        blk = full[kind].at[prow(core, y, 0, YROWS)]
        return remote(blk, blk, gys.at[kind, d - 1], gyr.at[kind, d - 1], ydev(d))

    def gy_recv(kind, d):
        dst = full[kind].at[prow(core, lax.rem(y + NY - d, NY), 0, YROWS)]
        return remote(dst, dst, gys.at[kind, d - 1], gyr.at[kind, d - 1], ydev(d))

    def gs(kind, d):
        blk = full[kind].at[prow(core, lax.rem(y + NY - d, NY), 0, YROWS)]
        return remote(blk, blk, gss.at[kind, d], gsr.at[kind, d], sib)

    def gs_recv(kind, d):
        dst = full[kind].at[prow(1 - core, lax.rem(y + NY - d, NY), 0, YROWS)]
        return remote(dst, dst, gss.at[kind, d], gsr.at[kind, d], sib)

    for kind in (0, 1):
        gz_local(kind).start()
    for kind in range(6):
        xlocal(kind).start()

    pl.semaphore_wait(barrier, len(peers))

    for kind in (0, 1):
        for d in range(1, NZ):
            gz(kind, d).start()
    for kind in (0, 2, 1, 3, 4, 5):
        for d in range(1, NX):
            xsend(kind, d).start()

    for kind in (0, 1):
        gz_local(kind).wait()
        for d in range(1, NZ):
            gz_recv(kind, d).wait_recv()
        for d in range(1, NY):
            gy(kind, d).start()
        gs(kind, 0).start()
    for kind in (0, 1):
        for d in range(1, NY):
            gy_recv(kind, d).wait_recv()
            gs(kind, d).start()
    for kind in (0, 1):
        for d in range(NY):
            gs_recv(kind, d).wait_recv()

    def arrive(kinds):
        for kind in kinds:
            xlocal(kind).wait()
            for d in range(1, NX):
                xrecv(kind, d).wait_recv()

    length = len_ref[0, 0]
    tok = lax.broadcasted_iota(jnp.int32, (RESP, 1), 0)
    weight = jnp.full((RESP, 1), adv_ref[0, 0], F32) / jnp.full((RESP, 1), length.astype(F32), F32)
    factor = jnp.where(tok < length, weight, 0.0)

    def seen():
        s = lax.broadcasted_iota(jnp.int32, (RESP, RESP), 0)
        t = lax.broadcasted_iota(jnp.int32, (RESP, RESP), 1)
        return (s <= t) & (s < length)

    nblk = KEYS // RESP

    def head(kv, h):
        lanes = slice(kv * D, (kv + 1) * D)
        rows = pl.ds(pl.multiple_of(h * RESP, RESP), RESP)
        qh = q_st[kv, rows]
        ch = c_st[kv, rows]
        top = None
        for b in range(nblk):
            kr = slice(b * RESP, (b + 1) * RESP)
            s = nt(k_all[kr, lanes], qh)
            if b == nblk - 1:
                s = jnp.where(seen(), s, -1e30)
            s_buf[kr] = s
            m = fold(s, jnp.max)
            top = m if top is None else jnp.maximum(top, m)
        top = jnp.max(top, axis=0, keepdims=True) * C2
        total = accum = None
        for b in range(nblk):
            kr = slice(b * RESP, (b + 1) * RESP)
            dpr = nt(v_all[kr, lanes], ch)
            e = jnp.exp2(s_buf[kr] * C2 - top)
            s_buf[kr] = e
            dp_buf[kr] = dpr
            t1 = fold(e, jnp.sum)
            t2 = fold(e * dpr, jnp.sum)
            total = t1 if total is None else total + t1
            accum = t2 if accum is None else accum + t2
        total = jnp.sum(total, axis=0, keepdims=True)
        accum = jnp.sum(accum, axis=0, keepdims=True)
        inv = 1.0 / total
        delta = accum * inv
        for b in range(nblk):
            kr = slice(b * RESP, (b + 1) * RESP)
            p = s_buf[kr] * inv
            p_all[kr, rows] = p.astype(BF16)
            ds_all[kr, rows] = (p * (dp_buf[kr] - delta)).astype(BF16)

    def rsib(kv):
        return remote(rs_snd.at[kv], rs_sib.at[kv], r0s.at[kv], r0r.at[kv], sib)

    def ry(kv, d):
        src = rs_ysnd.at[kv, pl.ds(pl.multiple_of(lax.rem(y + d, NY) * YROWS, YROWS), YROWS)]
        return remote(src, rs_y.at[kv, d - 1], r1s.at[kv, d - 1], r1r.at[kv, d - 1], ydev(d))

    def rz(kv, d):
        src = rs_zsnd.at[kv, pl.ds(pl.multiple_of(lax.rem(zh + d, NZ) * PIECE, PIECE), PIECE)]
        return remote(src, rs_z.at[kv, d - 1], r2s.at[kv, d - 1], r2r.at[kv, d - 1], zdev(d))

    def reduce_sib(kv):
        rsib(kv).wait_recv()
        own = rs_own[...] + rs_sib[kv].astype(F32)
        rs_own[...] = own
        rs_ysnd[kv] = own.astype(BF16)
        for d in range(1, NY):
            ry(kv, d).start()

    def reduce_y(kv):
        acc = rs_own[pl.ds(pl.multiple_of(y * YROWS, YROWS), YROWS)]
        for d in range(1, NY):
            ry(kv, d).wait_recv()
            acc = acc + rs_y[kv, d - 1].astype(F32)
        rs_zsum[...] = acc
        rs_zsnd[kv] = acc.astype(BF16)
        for d in range(1, NZ):
            rz(kv, d).start()

    def reduce_z(kv):
        acc = rs_zsum[pl.ds(pl.multiple_of(zh * PIECE, PIECE), PIECE)]
        for d in range(1, NZ):
            rz(kv, d).wait_recv()
            acc = acc + rs_z[kv, d - 1].astype(F32)
        dpk_v[:, kv * D : (kv + 1) * D] = acc[:, :D].astype(BF16)
        dpv_v[:, kv * D : (kv + 1) * D] = acc[:, D:].astype(BF16)

    def span(kv, lo, hi):
        def step(h, carry):
            head(kv, h)
            return carry

        lax.fori_loop(lo, hi, step, 0)

    b_own[...] = jnp.zeros_like(b_own)

    for kv in range(KV):
        lanes = slice(kv * D, (kv + 1) * D)
        arrive((0, 1, 2, 3) if kv == 0 else (4, 5))
        for h in range(RATIO):
            rows = slice(h * RESP, (h + 1) * RESP)
            q_st[kv, rows] = q_all[kv, :, h * D : (h + 1) * D]
            c_st[kv, rows] = (do_all[kv, :, h * D : (h + 1) * D].astype(F32) * factor).astype(BF16)
        k_t[...] = k_all[:, lanes].T
        if kv == 0:
            span(kv, 0, RATIO)
        else:
            span(kv, 0, 1)
            reduce_sib(kv - 1)
            span(kv, 1, 3)
            reduce_y(kv - 1)
            span(kv, 3, RATIO)
            reduce_z(kv - 1)
        other = pl.ds(pl.multiple_of((1 - core) * HALF, HALF), HALF)
        mine = pl.ds(pl.multiple_of(core * HALF, HALF), HALF)
        rs_snd[kv, :, :D] = (nn(ds_all[other], q_st[kv]) * SCALE).astype(BF16)
        rs_snd[kv, :, D:] = nn(p_all[other], c_st[kv]).astype(BF16)
        rsib(kv).start()
        rs_own[:, :D] = nn(ds_all[mine], q_st[kv]) * SCALE
        rs_own[:, D:] = nn(p_all[mine], c_st[kv])
        if kv == KV - 1:
            reduce_sib(kv)
        dks = nn(ds_all[PRE:], q_st[kv]) * SCALE
        dvs = nn(p_all[PRE:], c_st[kv])
        dks_v[:, lanes] = dks.astype(BF16)
        dvs_v[:, lanes] = dvs.astype(BF16)
        b_own[KV * RATIO + kv : KV * RATIO + kv + 1] = jnp.sum(dks, axis=0, keepdims=True)
        b_own[KV * RATIO + KV + kv : KV * RATIO + KV + kv + 1] = jnp.sum(dvs, axis=0, keepdims=True)
        for h in range(RATIO):
            dqh = (nn(k_t[...], ds_all[:, h * RESP : (h + 1) * RESP]) * SCALE).T
            r = kv * RATIO + h
            dq_v[:, r * D : (r + 1) * D] = dqh.astype(BF16)
            b_own[r : r + 1] = jnp.sum(dqh, axis=0, keepdims=True)

    outs = [
        pltpu.make_async_copy(dq_v, dq_out, osem.at[0]),
        pltpu.make_async_copy(dks_v, dks_out, osem.at[1]),
        pltpu.make_async_copy(dvs_v, dvs_out, osem.at[2]),
    ]
    for copy in outs:
        copy.start()

    bsib = remote(b_own, b_sib, bs0, br0, sib)
    bsib.start()
    reduce_y(KV - 1)
    bsib.wait_recv()
    b_y[pl.ds(y, 1)] = (b_own[...] + b_sib[...])[None]

    def by(d):
        return remote(b_y.at[y], b_y.at[y], bs1.at[d - 1], br1.at[d - 1], ydev(d))

    def by_recv(d):
        dst = b_y.at[lax.rem(y + NY - d, NY)]
        return remote(dst, dst, bs1.at[d - 1], br1.at[d - 1], ydev(d))

    for d in range(1, NY):
        by(d).start()
    reduce_z(KV - 1)
    for d in range(1, NY):
        by_recv(d).wait_recv()
    acc = b_y[0]
    for i in range(1, NY):
        acc = acc + b_y[i]
    b_z[pl.ds(zpos, 1)] = acc[None]

    def bz(d):
        return remote(b_z.at[zpos], b_z.at[zpos], bs2.at[d - 1], br2.at[d - 1], zzdev(d))

    def bz_recv(d):
        dst = b_z.at[lax.rem(zpos + 2 * NZ - d, 2 * NZ)]
        return remote(dst, dst, bs2.at[d - 1], br2.at[d - 1], zzdev(d))

    for d in range(1, 2 * NZ):
        bz(d).start()
    tail = [
        pltpu.make_async_copy(dpk_v, dpk_out, osem.at[3]),
        pltpu.make_async_copy(dpv_v, dpv_out, osem.at[4]),
    ]
    for copy in tail:
        copy.start()
    for d in range(1, 2 * NZ):
        bz_recv(d).wait_recv()
    acc = b_z[0]
    for i in range(1, 2 * NZ):
        acc = acc + b_z[i]
    nq = KV * RATIO
    qb_v[...] = acc[:nq]
    for kv in range(KV):
        kvb_v[0:1, kv * D : (kv + 1) * D] = acc[nq + kv : nq + kv + 1]
        kvb_v[1:2, kv * D : (kv + 1) * D] = acc[nq + KV + kv : nq + KV + kv + 1]
    tail2 = [
        pltpu.make_async_copy(qb_v, qb_out, osem.at[5]),
        pltpu.make_async_copy(kvb_v, kvb_out, osem.at[6]),
    ]
    for copy in tail2:
        copy.start()

    for kind in range(6):
        for d in range(1, NX):
            xsend(kind, d).wait_send()
    for kind in (0, 1):
        for d in range(1, NZ):
            gz(kind, d).wait_send()
        for d in range(1, NY):
            gy(kind, d).wait_send()
        for d in range(NY):
            gs(kind, d).wait_send()
    for kv in range(KV):
        rsib(kv).wait_send()
        for d in range(1, NY):
            ry(kv, d).wait_send()
        for d in range(1, NZ):
            rz(kv, d).wait_send()
    bsib.wait_send()
    for d in range(1, NY):
        by(d).wait_send()
    for d in range(1, 2 * NZ):
        bz(d).wait_send()
    for copy in outs + tail + tail2:
        copy.wait()


def local(queries, suffix_keys, suffix_values, d_out, prefix_keys, prefix_values, advantages, lengths):
    sds = jax.ShapeDtypeStruct
    dma = pltpu.SemaphoreType.DMA
    hbm = pl.BlockSpec(memory_space=pl.ANY)
    smem = pl.BlockSpec(memory_space=pltpu.SMEM)
    nb = KV * RATIO
    vm = pltpu.VMEM
    out = pl.pallas_call(
        kernel,
        out_shape=(
            sds((RESP, KV * QC), BF16),
            sds((RESP, KV * D), BF16),
            sds((RESP, KV * D), BF16),
            sds((PIECE, KV * D), BF16),
            sds((PIECE, KV * D), BF16),
            sds((nb, D), F32),
            sds((2, KV * D), F32),
        ),
        in_specs=[hbm] * 6 + [smem] * 2,
        out_specs=(hbm,) * 7,
        scratch_shapes=[
            vm((KV, RESP, QC), BF16), vm((KV, RESP, QC), BF16),
            vm((KEYS, KV * D), BF16), vm((KEYS, KV * D), BF16),
            vm((D, KEYS), BF16),
            vm((KV, QT, D), BF16), vm((KV, QT, D), BF16),
            vm((KEYS, RESP), F32), vm((KEYS, RESP), F32),
            vm((KEYS, QT), BF16), vm((KEYS, QT), BF16),
            vm((RESP, KV * QC), BF16), vm((RESP, KV * D), BF16), vm((RESP, KV * D), BF16),
            vm((KV, HALF, 2 * D), BF16), vm((KV, HALF, 2 * D), BF16), vm((HALF, 2 * D), F32),
            vm((KV, HALF, 2 * D), BF16), vm((KV, NY - 1, YROWS, 2 * D), BF16),
            vm((YROWS, 2 * D), F32), vm((KV, YROWS, 2 * D), BF16),
            vm((KV, NZ - 1, PIECE, 2 * D), BF16), vm((PIECE, KV * D), BF16), vm((PIECE, KV * D), BF16),
            vm((16, D), F32), vm((16, D), F32), vm((NY, 16, D), F32), vm((2 * NZ, 16, D), F32),
            vm((nb, D), F32), vm((2, KV * D), F32),
            dma((6, NX - 1)), dma((6, NX - 1)), dma((6,)),
            dma((2, NZ - 1)), dma((2, NZ - 1)), dma((2,)),
            dma((2, NY - 1)), dma((2, NY - 1)), dma((2, NY)), dma((2, NY)),
            dma((KV,)), dma((KV,)), dma((KV, NY - 1)), dma((KV, NY - 1)), dma((KV, NZ - 1)), dma((KV, NZ - 1)),
            dma, dma, dma((NY - 1,)), dma((NY - 1,)), dma((2 * NZ - 1,)), dma((2 * NZ - 1,)),
            dma((7,)),
        ],
        compiler_params=pltpu.CompilerParams(
            collective_id=0, has_side_effects=True, vmem_limit_bytes=48 * 1024 * 1024
        ),
        name="grouped_attention_backward",
    )(
        queries[0, 0], suffix_keys[0, 0], suffix_values[0, 0], d_out[0, 0],
        prefix_keys[0], prefix_values[0], advantages, lengths,
    )
    dq, dks, dvs, dpk, dpv, qb, kvb = out
    return (dq[None, None], dks[None, None], dvs[None, None], dpk[None], dpv[None], qb.reshape(-1), kvb)


def solution(mesh):
    in_specs = (
        P("dp", "group", "tensor", None),
        P("dp", "group", "tensor", None),
        P("dp", "group", "tensor", None),
        P("dp", "group", "tensor", None),
        P("dp", "group", "tensor"),
        P("dp", "group", "tensor"),
        P("dp", "group"),
        P("dp", "group"),
    )
    out_specs = (
        P("dp", "group", None, "tensor"),
        P("dp", "group", None, "tensor"),
        P("dp", "group", None, "tensor"),
        P("dp", "group", "tensor"),
        P("dp", "group", "tensor"),
        P("tensor"),
        P(None, "tensor"),
    )
    return jax.shard_map(local, mesh=mesh, in_specs=in_specs, out_specs=out_specs, check_vma=False)
```

time: 544 us -> 72.1 us (0.13)
  the two profiles are of different devices: /device:TPU:4 before, /device:TPU:1 now
where the time goes in v1:
time: 72.1 us; the launch traced here: 71.4 us
  Pallas kernels  59.5 us (83%)
  local copies, waits for them, and re-layouts  9.94 us (14%)
  between operations  1.95 us (3%)
    pallas_call x1, Pallas kernels, local(): pl.pallas_call(kernel, out_shape=(sds((RESP, KV * QC), BF16), sds((RESP,...  59.5 us
    unnamed x19, local copies, waits for them, and re-layouts  9.94 us

profile of v1, /device:TPU:1, one launch (start us, length us, event | category | flops | bytes accessed | tf_op | source)
XLA Modules:
  0.0 71.4 jit_solution(3522607913469288871)
XLA Ops:
  1.9 0.0 copy-start
  1.9 1.1 %copy-done = bf16[1,1,64,5120]{3,2,1,0:T(8,128)(2,1)S(1)} copy-done((bf16[1,1,64,5120]{3,2,1,0:T(8,128)(2,1)S(1)}, bf16[1,1,64,5120]{3,2,1,0:T(8,128)(2,1)}, u32[]{:S(2)}) %copy-start) | copy-done | bytes 655384
  3.0 0.0 copy-start.1
  3.0 1.1 %copy-done.1 = bf16[1,1,64,5120]{3,2,1,0:T(8,128)(2,1)S(1)} copy-done((bf16[1,1,64,5120]{3,2,1,0:T(8,128)(2,1)S(1)}, bf16[1,1,64,5120]{3,2,1,0:T(8,128)(2,1)}, u32[]{:S(2)}) %copy-start.1) | copy-done | bytes 655384
  4.1 0.0 copy-start.2
  4.1 0.9 %copy-done.2 = bf16[1,1,64,1024]{3,2,1,0:T(8,128)(2,1)S(1)} copy-done((bf16[1,1,64,1024]{3,2,1,0:T(8,128)(2,1)S(1)}, bf16[1,1,64,1024]{3,2,1,0:T(8,128)(2,1)}, u32[]{:S(2)}) %copy-start.2) | copy-done | bytes 131096
  5.0 0.0 copy-start.3
  5.0 0.9 %copy-done.3 = bf16[1,1,64,1024]{3,2,1,0:T(8,128)(2,1)S(1)} copy-done((bf16[1,1,64,1024]{3,2,1,0:T(8,128)(2,1)S(1)}, bf16[1,1,64,1024]{3,2,1,0:T(8,128)(2,1)}, u32[]{:S(2)}) %copy-start.3) | copy-done | bytes 131096
  5.9 0.0 copy-start.4
  5.9 0.7 %copy-done.4 = bf16[1,32,256]{2,1,0:T(8,128)(2,1)S(1)} copy-done((bf16[1,32,256]{2,1,0:T(8,128)(2,1)S(1)}, bf16[1,32,256]{2,1,0:T(8,128)(2,1)}, u32[]{:S(2)}) %copy-start.4) | copy-done | bytes 16408
  6.6 0.0 copy-start.5
  6.6 0.7 %copy-done.5 = bf16[1,32,256]{2,1,0:T(8,128)(2,1)S(1)} copy-done((bf16[1,32,256]{2,1,0:T(8,128)(2,1)S(1)}, bf16[1,32,256]{2,1,0:T(8,128)(2,1)}, u32[]{:S(2)}) %copy-start.5) | copy-done | bytes 16408
  7.3 59.5 %grouped_attention_backward.1 = (bf16[256,1280]{1,0:T(8,128)(2,1)S(1)}, bf16[256,256]{1,0:T(8,128)(2,1)S(1)}, bf16[256,256]{1,0:T(8,128)(2,1)S(1)}, bf16[32,256]...) custom-call(bf16[64,5120]{1,0:T(8,128)(2,1)S(1)} %bitcast.12, ...), custom_call_target="tpu_custom_call" | custom-call | tf_op jit(solution)/shard_map/grouped_attention_backward/pallas_call | solution.py:418
  66.8 0.8 %copy.24 = bf16[1,1,256,1280]{3,2,1,0:T(8,128)(2,1)} copy(bf16[1,1,256,1280]{3,2,1,0:T(8,128)(2,1)S(1)} %bitcast.14) | data formatting | bytes 1310720
  67.7 0.7 copy.25
  68.3 0.7 copy.26
  69.0 0.6 copy.27
  69.6 0.6 copy.28
  70.2 0.6 copy.29
  70.8 0.6 copy.30
Async XLA Ops:
  1.9 1.1 %copy-start = (bf16[1,1,64,5120]{3,2,1,0:T(8,128)(2,1)S(1)}, bf16[1,1,64,5120]{3,2,1,0:T(8,128)(2,1)}, u32[]{:S(2)}) copy-start(bf16[1,1,64,5120]{3,2,1,0:T(8,128)(2,1)} %param.8) | copy-start | bytes 1966084
  3.0 1.1 %copy-start.1 = (bf16[1,1,64,5120]{3,2,1,0:T(8,128)(2,1)S(1)}, bf16[1,1,64,5120]{3,2,1,0:T(8,128)(2,1)}, u32[]{:S(2)}) copy-start(bf16[1,1,64,5120]{3,2,1,0:T(8,128)(2,1)} %param.11) | copy-start | bytes 1966084
  4.1 0.9 %copy-start.2 = (bf16[1,1,64,1024]{3,2,1,0:T(8,128)(2,1)S(1)}, bf16[1,1,64,1024]{3,2,1,0:T(8,128)(2,1)}, u32[]{:S(2)}) copy-start(bf16[1,1,64,1024]{3,2,1,0:T(8,128)(2,1)} %param.9) | copy-start | bytes 393220
  5.0 0.9 %copy-start.3 = (bf16[1,1,64,1024]{3,2,1,0:T(8,128)(2,1)S(1)}, bf16[1,1,64,1024]{3,2,1,0:T(8,128)(2,1)}, u32[]{:S(2)}) copy-start(bf16[1,1,64,1024]{3,2,1,0:T(8,128)(2,1)} %param.10) | copy-start | bytes 393220
  5.9 0.7 %copy-start.4 = (bf16[1,32,256]{2,1,0:T(8,128)(2,1)S(1)}, bf16[1,32,256]{2,1,0:T(8,128)(2,1)}, u32[]{:S(2)}) copy-start(bf16[1,32,256]{2,1,0:T(8,128)(2,1)} %param.12) | copy-start | bytes 49156
  6.6 0.7 %copy-start.5 = (bf16[1,32,256]{2,1,0:T(8,128)(2,1)S(1)}, bf16[1,32,256]{2,1,0:T(8,128)(2,1)}, u32[]{:S(2)}) copy-start(bf16[1,32,256]{2,1,0:T(8,128)(2,1)} %param.13) | copy-start | bytes 49156

commit v2 on v1

v2 whole, which is shorter than its diff:
```python
import math

import jax
import jax.numpy as jnp
from jax import lax
from jax.experimental import pallas as pl
from jax.experimental.pallas import tpu as pltpu
from jax.sharding import PartitionSpec as P

H = 40
KEY_VALUE_HEADS = 8
D = 128
RATIO = H // KEY_VALUE_HEADS
NX = 4
NY = 4
NZ = 4
KV = KEY_VALUE_HEADS // NX
TOK = 64
RESP = NX * TOK
QC = RATIO * D
PRE = 1024
KEYS = PRE + RESP
PIECE = PRE // (2 * NY * NZ)
YROWS = NZ * PIECE
HALF = NY * YROWS
QT = RATIO * RESP
SCALE = D ** -0.5
C2 = SCALE * math.log2(math.e)
MESH = pl.DeviceIdType.MESH
F32 = jnp.float32
BF16 = jnp.bfloat16


def nt(a, b):
    return lax.dot_general(a, b, (((1,), (1,)), ((), ())), preferred_element_type=F32)


def nn(a, b):
    return lax.dot_general(a, b, (((1,), (0,)), ((), ())), preferred_element_type=F32)


def fold(a, op):
    return op(a.reshape(a.shape[0] // 8, 8, a.shape[1]), axis=0)


def kernel(
    q_in, ks_in, vs_in, do_in, pk_in, pv_in, adv_ref, len_ref,
    dq_out, dks_out, dvs_out, dpk_out, dpv_out, qb_out, kvb_out,
    q_st, do_st, c_st, kv_all, k_t, s_buf, dp_buf, p_all, ds_all,
    dq_v, dks_v, dvs_v, rs_snd, rs_sib, rs_own, rs_ysnd, rs_y, rs_zsum, rs_zsnd, rs_z, dpk_v, dpv_v,
    b_y, b_z, qb_v, kvb_v,
    xs, xr, kvs, kvr, gl, gzs, gzr, gys, gyr, gss, gsr,
    r0s, r0r, r1s, r1r, r2s, r2r, bs1, br1, bs2, br2, osem,
):
    g = lax.axis_index("group")
    x = lax.axis_index("tensor")
    dp = lax.axis_index("dp")
    core = lax.rem(g, 2)
    zh = lax.rem(g // 2, NZ)
    y = g // (2 * NZ)
    sib = {"group": g + 1 - 2 * core}

    def xdev(d):
        return {"tensor": lax.rem(x + d, NX)}

    def ydev(d):
        return {"group": lax.rem(y + d, NY) * (2 * NZ) + zh * 2 + core}

    def zdev(d):
        return {"group": y * (2 * NZ) + lax.rem(zh + d, NZ) * 2 + core}

    ypos = y * 2 + core
    zpos = zh * 2 + dp

    def yydev(d):
        p = lax.rem(ypos + d, 2 * NY)
        return {"group": (p // 2) * (2 * NZ) + zh * 2 + lax.rem(p, 2)}

    def zzdev(d):
        p = lax.rem(zpos + d, 2 * NZ)
        return {"group": y * (2 * NZ) + (p // 2) * 2 + core, "dp": lax.rem(p, 2)}

    def remote(src, dst, ss, rs, dev):
        return pltpu.make_async_remote_copy(
            src_ref=src, dst_ref=dst, send_sem=ss, recv_sem=rs, device_id=dev, device_id_type=MESH
        )

    def await_recv(ref, sem):
        remote(ref, ref, osem.at[0], sem, sib).wait_recv()

    def await_send(ref, sem):
        remote(ref, ref, sem, osem.at[0], sib).wait_send()

    barrier = pltpu.get_barrier_semaphore()
    peers = [xdev(d) for d in range(1, NX)] + [yydev(d) for d in range(1, 2 * NY)]
    peers += [zzdev(d) for d in range(1, 2 * NZ)]
    for dev in peers:
        pl.semaphore_signal(barrier, inc=1, device_id=dev, device_id_type=MESH)

    def xsrc(kind, owner, r):
        return (q_in, do_in)[kind].at[:, pl.ds(pl.multiple_of((owner * KV * RATIO + r) * D, D), D)]

    def xdst(kind, source, r):
        return (q_st, do_st)[kind].at[pl.ds(pl.multiple_of(r * RESP + source * TOK, TOK), TOK)]

    def ksrc(kind, owner, kv):
        return (ks_in, vs_in)[kind].at[:, pl.ds(pl.multiple_of((owner * KV + kv) * D, D), D)]

    def kdst(kind, source, kv):
        return kv_all.at[kv, pl.ds(pl.multiple_of(PRE + source * TOK, TOK), TOK), kind * D : (kind + 1) * D]

    def start_head(r):
        for kind in (0, 1):
            for d in (2, 1, 3):
                src = xsrc(kind, lax.rem(x + d, NX), r)
                remote(src, xdst(kind, x, r), xs.at[kind], xr.at[kind, r], xdev(d)).start()

    def start_keys(kv):
        for kind in (0, 1):
            for d in (2, 1, 3):
                src = ksrc(kind, lax.rem(x + d, NX), kv)
                remote(src, kdst(kind, x, kv), kvs, kvr.at[kv], xdev(d)).start()

    def prow(c, zz, yy, n=PIECE):
        return pl.ds(pl.multiple_of(c * HALF + zz * YROWS + yy * PIECE, PIECE), n)

    def from_z(e):
        return lax.rem(zh + NZ - e, NZ)

    def gather_z(kv):
        own = kv_all.at[kv, prow(core, zh, y)]
        for d in (2, 1, 3):
            remote(own, own, gzs.at[kv], gzr.at[kv, d - 1], zdev(d)).start()

    def gather_y(kv, e):
        blk = kv_all.at[kv, prow(core, from_z(e), y)]
        if e > 0:
            await_recv(blk, gzr.at[kv, e - 1])
        for d in (2, 1, 3):
            remote(blk, blk, gys.at[kv], gyr.at[kv, e], ydev(d)).start()

    def gather_sib(kv, e):
        await_recv(kv_all.at[kv, 0 : (NY - 1) * PIECE], gyr.at[kv, e])
        blk = kv_all.at[kv, prow(core, from_z(e), 0, YROWS)]
        remote(blk, blk, gss.at[kv], gsr.at[kv], sib).start()

    def gather_done(kv):
        await_recv(kv_all.at[kv, 0:HALF], gsr.at[kv])

    for kv in range(KV):
        for kind in (0, 1):
            dst = kv_all.at[kv, prow(core, zh, y), kind * D : (kind + 1) * D]
            pltpu.make_async_copy((pk_in, pv_in)[kind].at[:, kv * D : (kv + 1) * D], dst, gl.at[kv]).start()
    for kv in range(KV):
        await_recv(kv_all.at[kv, 0:PIECE], gl.at[kv])

    pl.semaphore_wait(barrier, len(peers))

    gather_z(0)
    gather_y(0, 0)
    start_head(0)
    start_keys(0)
    gather_z(1)
    gather_y(1, 0)
    for h in range(1, RATIO):
        start_head(h)
    for r in range(KV * RATIO):
        for kind in (0, 1):
            pltpu.make_async_copy(xsrc(kind, x, r), xdst(kind, x, r), xr.at[kind, r]).start()
    for kv in range(KV):
        for kind in (0, 1):
            pltpu.make_async_copy(ksrc(kind, x, kv), kdst(kind, x, kv), kvr.at[kv]).start()
    order = (1, 3, 2)
    for e in order:
        gather_y(0, e)
    start_keys(1)
    start_head(RATIO)
    for e in order:
        gather_y(1, e)
    start_head(RATIO + 1)
    for e in (0,) + order:
        gather_sib(0, e)
    for h in range(2, RATIO):
        start_head(RATIO + h)
    gather_done(0)

    length = len_ref[0, 0]
    tok = lax.broadcasted_iota(jnp.int32, (RESP, 1), 0)
    weight = jnp.full((RESP, 1), adv_ref[0, 0], F32) / jnp.full((RESP, 1), length.astype(F32), F32)
    factor = jnp.where(tok < length, weight, 0.0)

    def seen():
        s = lax.broadcasted_iota(jnp.int32, (RESP, RESP), 0)
        t = lax.broadcasted_iota(jnp.int32, (RESP, RESP), 1)
        return (s <= t) & (s < length)

    nblk = KEYS // RESP

    def head(kv, h):
        rows = pl.ds(pl.multiple_of(h * RESP, RESP), RESP)
        r = kv * RATIO + h
        all_rows = pl.ds(pl.multiple_of(r * RESP, RESP), RESP)
        for kind in (0, 1):
            await_recv((q_st, do_st)[kind].at[all_rows], xr.at[kind, r])
        qh = q_st[all_rows]
        ch = (do_st[all_rows].astype(F32) * factor).astype(BF16)
        c_st[all_rows] = ch
        top = None
        for b in range(nblk):
            kr = slice(b * RESP, (b + 1) * RESP)
            s = nt(kv_all[kv, kr, :D], qh)
            if b == nblk - 1:
                s = jnp.where(seen(), s, -1e30)
            s_buf[kr] = s
            m = fold(s, jnp.max)
            top = m if top is None else jnp.maximum(top, m)
        top = jnp.max(top, axis=0, keepdims=True) * C2
        total = accum = None
        for b in range(nblk):
            kr = slice(b * RESP, (b + 1) * RESP)
            dpr = nt(kv_all[kv, kr, D:], ch)
            e = jnp.exp2(s_buf[kr] * C2 - top)
            s_buf[kr] = e
            dp_buf[kr] = dpr
            t1 = fold(e, jnp.sum)
            t2 = fold(e * dpr, jnp.sum)
            total = t1 if total is None else total + t1
            accum = t2 if accum is None else accum + t2
        total = jnp.sum(total, axis=0, keepdims=True)
        accum = jnp.sum(accum, axis=0, keepdims=True)
        inv = 1.0 / total
        delta = accum * inv
        for b in range(nblk):
            kr = slice(b * RESP, (b + 1) * RESP)
            p = s_buf[kr] * inv
            p_all[kr, rows] = p.astype(BF16)
            ds_all[kr, rows] = (p * (dp_buf[kr] - delta)).astype(BF16)

    def rsib(kv):
        return remote(rs_snd.at[kv], rs_sib.at[kv], r0s.at[kv], r0r.at[kv], sib)

    far = (2, 1, 3, 0)

    def to_z(e):
        return lax.rem(zh + e, NZ)

    def zrows(e):
        return pl.ds(pl.multiple_of(to_z(e) * YROWS, YROWS), YROWS)

    def zyrows(e, d):
        return pl.ds(pl.multiple_of(to_z(e) * YROWS + lax.rem(y + d, NY) * PIECE, PIECE), PIECE)

    def reduce_sib(kv):
        rsib(kv).wait_recv()
        for e in far:
            own = rs_own[zrows(e)] + rs_sib[kv, zrows(e)].astype(F32)
            rs_own[zrows(e)] = own
            rs_ysnd[kv, zrows(e)] = own.astype(BF16)
            for d in (2, 1, 3):
                src = rs_ysnd.at[kv, zyrows(e, d)]
                remote(src, rs_y.at[kv, e, d - 1], r1s.at[kv], r1r.at[kv, e], ydev(d)).start()

    def reduce_y(kv):
        for e in far:
            await_recv(rs_y.at[kv, e], r1r.at[kv, e])
            acc = rs_own[zyrows(e, 0)]
            for d in range(1, NY):
                acc = acc + rs_y[kv, e, d - 1].astype(F32)
            if e == 0:
                rs_zsum[...] = acc
            else:
                rs_zsnd[kv, e - 1] = acc.astype(BF16)
                remote(rs_zsnd.at[kv, e - 1], rs_z.at[kv, e - 1], r2s.at[kv], r2r.at[kv], zdev(e)).start()

    def reduce_z(kv):
        await_recv(rs_z.at[kv], r2r.at[kv])
        acc = rs_zsum[...]
        for d in range(1, NZ):
            acc = acc + rs_z[kv, d - 1].astype(F32)
        dpk_v[:, kv * D : (kv + 1) * D] = acc[:, :D].astype(BF16)
        dpv_v[:, kv * D : (kv + 1) * D] = acc[:, D:].astype(BF16)

    def span(kv, lo, hi):
        def step(h, carry):
            head(kv, h)
            return carry

        lax.fori_loop(lo, hi, step, 0)

    nb = KV * RATIO
    biases = [None] * 16
    outs = []
    for kv in range(KV):
        lanes = slice(kv * D, (kv + 1) * D)
        if kv > 0:
            gather_done(kv)
        await_recv(kv_all.at[kv, PRE:KEYS], kvr.at[kv])
        k_t[...] = kv_all[kv, :, :D].T
        if kv == 0:
            span(kv, 0, 1)
            for e in (0,) + order:
                gather_sib(1, e)
            span(kv, 1, RATIO)
        else:
            span(kv, 0, 1)
            reduce_sib(kv - 1)
            span(kv, 1, 3)
            reduce_y(kv - 1)
            span(kv, 3, RATIO)
            reduce_z(kv - 1)
        qs = slice(kv * QT, (kv + 1) * QT)
        other = pl.ds(pl.multiple_of((1 - core) * HALF, HALF), HALF)
        mine = pl.ds(pl.multiple_of(core * HALF, HALF), HALF)
        rs_snd[kv, :, :D] = (nn(ds_all[other], q_st[qs]) * SCALE).astype(BF16)
        rs_snd[kv, :, D:] = nn(p_all[other], c_st[qs]).astype(BF16)
        rsib(kv).start()
        rs_own[:, :D] = nn(ds_all[mine], q_st[qs]) * SCALE
        rs_own[:, D:] = nn(p_all[mine], c_st[qs])
        if kv == KV - 1:
            reduce_sib(kv)
        dks = nn(ds_all[PRE:], q_st[qs]) * SCALE
        dvs = nn(p_all[PRE:], c_st[qs])
        dks_v[:, lanes] = dks.astype(BF16)
        dvs_v[:, lanes] = dvs.astype(BF16)
        b_y[ypos, nb + kv : nb + kv + 1] = jnp.sum(dks, axis=0, keepdims=True)
        b_y[ypos, nb + KV + kv : nb + KV + kv + 1] = jnp.sum(dvs, axis=0, keepdims=True)
        for h in range(RATIO):
            dqh = (nn(k_t[...], ds_all[:, h * RESP : (h + 1) * RESP]) * SCALE).T
            r = kv * RATIO + h
            dq_v[:, r * D : (r + 1) * D] = dqh.astype(BF16)
            b_y[ypos, r : r + 1] = jnp.sum(dqh, axis=0, keepdims=True)
        copy = pltpu.make_async_copy(
            dq_v.at[:, kv * QC : (kv + 1) * QC], dq_out.at[:, kv * QC : (kv + 1) * QC], osem.at[7 + kv]
        )
        copy.start()
        outs.append(copy)

    b_y[ypos, nb + 2 * KV :] = jnp.zeros((16 - nb - 2 * KV, D), F32)
    for d in range(1, 2 * NY):
        remote(b_y.at[ypos], b_y.at[ypos], bs1, br1, yydev(d)).start()
    for src, dst, i in ((dks_v, dks_out, 1), (dvs_v, dvs_out, 2)):
        copy = pltpu.make_async_copy(src, dst, osem.at[i])
        copy.start()
        outs.append(copy)
    reduce_y(KV - 1)
    await_recv(b_y.at[0 : 2 * NY - 1], br1)
    acc = b_y[0]
    for i in range(1, 2 * NY):
        acc = acc + b_y[i]
    b_z[pl.ds(zpos, 1)] = acc[None]
    for d in range(1, 2 * NZ):
        remote(b_z.at[zpos], b_z.at[zpos], bs2, br2, zzdev(d)).start()
    reduce_z(KV - 1)
    for src, dst, i in ((dpk_v, dpk_out, 3), (dpv_v, dpv_out, 4)):
        copy = pltpu.make_async_copy(src, dst, osem.at[i])
        copy.start()
        outs.append(copy)

    for kind in (0, 1):
        await_send(q_st.at[0 : KV * RATIO * (NX - 1) * TOK], xs.at[kind])
    await_send(q_st.at[0 : 2 * KV * (NX - 1) * TOK], kvs)
    for kv in range(KV):
        await_send(kv_all.at[kv, 0 : (NZ - 1) * PIECE], gzs.at[kv])
        await_send(kv_all.at[kv, 0 : NZ * (NY - 1) * PIECE], gys.at[kv])
        await_send(kv_all.at[kv, 0:HALF], gss.at[kv])
        rsib(kv).wait_send()
        await_send(kv_all.at[kv, 0 : NZ * (NY - 1) * PIECE], r1s.at[kv])
        await_send(rs_z.at[kv], r2s.at[kv])
    await_send(b_y.at[0 : 2 * NY - 1], bs1)

    await_recv(b_z.at[0 : 2 * NZ - 1], br2)
    acc = b_z[0]
    for i in range(1, 2 * NZ):
        acc = acc + b_z[i]
    qb_v[...] = acc[:nb]
    for kv in range(KV):
        kvb_v[0:1, kv * D : (kv + 1) * D] = acc[nb + kv : nb + kv + 1]
        kvb_v[1:2, kv * D : (kv + 1) * D] = acc[nb + KV + kv : nb + KV + kv + 1]
    for src, dst, i in ((qb_v, qb_out, 5), (kvb_v, kvb_out, 6)):
        copy = pltpu.make_async_copy(src, dst, osem.at[i])
        copy.start()
        outs.append(copy)
    await_send(b_z.at[0 : 2 * NZ - 1], bs2)
    for copy in outs:
        copy.wait()


def finish(*refs):
    n = (len(refs) - 2) // 3
    sem_in, sem_out = refs[-2:]
    first, second = [], []
    for i in range(n):
        src, dst, held = refs[i], refs[n + i], refs[2 * n + i]
        parts = 4 if i == 0 else 1
        step = src.shape[0] // parts
        for j in range(parts):
            rows = pl.ds(j * step, step)
            k = len(first)
            first.append(pltpu.make_async_copy(src.at[rows], held.at[rows], sem_in.at[k]))
            second.append(pltpu.make_async_copy(held.at[rows], dst.at[rows], sem_out.at[k]))
    for copy in first:
        copy.start()
    for a, b in zip(first, second):
        a.wait()
        b.start()
    for copy in second:
        copy.wait()


def local(queries, suffix_keys, suffix_values, d_out, prefix_keys, prefix_values, advantages, lengths):
    sds = jax.ShapeDtypeStruct
    dma = pltpu.SemaphoreType.DMA
    hbm = pl.BlockSpec(memory_space=pl.ANY)
    smem = pl.BlockSpec(memory_space=pltpu.SMEM)
    nb = KV * RATIO
    vm = pltpu.VMEM
    shapes = (
        sds((RESP, KV * QC), BF16),
        sds((RESP, KV * D), BF16),
        sds((RESP, KV * D), BF16),
        sds((PIECE, KV * D), BF16),
        sds((PIECE, KV * D), BF16),
        sds((nb, D), F32),
        sds((2, KV * D), F32),
    )
    out = pl.pallas_call(
        kernel,
        out_shape=shapes,
        in_specs=[hbm] * 6 + [smem] * 2,
        out_specs=(hbm,) * 7,
        scratch_shapes=[
            vm((KV * QT, D), BF16), vm((KV * QT, D), BF16), vm((KV * QT, D), BF16),
            vm((KV, KEYS, 2 * D), BF16),
            vm((D, KEYS), BF16),
            vm((KEYS, RESP), F32), vm((KEYS, RESP), F32),
            vm((KEYS, QT), BF16), vm((KEYS, QT), BF16),
            vm((RESP, KV * QC), BF16), vm((RESP, KV * D), BF16), vm((RESP, KV * D), BF16),
            vm((KV, HALF, 2 * D), BF16), vm((KV, HALF, 2 * D), BF16), vm((HALF, 2 * D), F32),
            vm((KV, HALF, 2 * D), BF16), vm((KV, NZ, NY - 1, PIECE, 2 * D), BF16),
            vm((PIECE, 2 * D), F32), vm((KV, NZ - 1, PIECE, 2 * D), BF16),
            vm((KV, NZ - 1, PIECE, 2 * D), BF16), vm((PIECE, KV * D), BF16), vm((PIECE, KV * D), BF16),
            vm((2 * NY, 16, D), F32), vm((2 * NZ, 16, D), F32),
            vm((nb, D), F32), vm((2, KV * D), F32),
            dma((2,)), dma((2, nb)), dma, dma((KV,)), dma((KV,)),
            dma((KV,)), dma((KV, NZ - 1)), dma((KV,)), dma((KV, NZ)), dma((KV,)), dma((KV,)),
            dma((KV,)), dma((KV,)), dma((KV,)), dma((KV, NZ)), dma((KV,)), dma((KV,)),
            dma, dma, dma, dma,
            dma((9,)),
        ],
        compiler_params=pltpu.CompilerParams(
            collective_id=0, has_side_effects=True, vmem_limit_bytes=60 * 1024 * 1024
        ),
        name="grouped_attention_backward",
    )(
        queries[0, 0], suffix_keys[0, 0], suffix_values[0, 0], d_out[0, 0],
        prefix_keys[0], prefix_values[0], advantages, lengths,
    )
    out = pl.pallas_call(
        finish,
        out_shape=shapes,
        in_specs=[hbm] * 7,
        out_specs=(hbm,) * 7,
        scratch_shapes=[vm(s.shape, s.dtype) for s in shapes] + [dma((10,)), dma((10,))],
        compiler_params=pltpu.CompilerParams(vmem_limit_bytes=60 * 1024 * 1024),
        name="finish",
    )(*out)
    dq, dks, dvs, dpk, dpv, qb, kvb = out
    return (dq[None, None], dks[None, None], dvs[None, None], dpk[None], dpv[None], qb.reshape(-1), kvb)


def solution(mesh):
    in_specs = (
        P("dp", "group", "tensor", None),
        P("dp", "group", "tensor", None),
        P("dp", "group", "tensor", None),
        P("dp", "group", "tensor", None),
        P("dp", "group", "tensor"),
        P("dp", "group", "tensor"),
        P("dp", "group"),
        P("dp", "group"),
    )
    out_specs = (
        P("dp", "group", None, "tensor"),
        P("dp", "group", None, "tensor"),
        P("dp", "group", None, "tensor"),
        P("dp", "group", "tensor"),
        P("dp", "group", "tensor"),
        P("tensor"),
        P(None, "tensor"),
    )
    return jax.shard_map(local, mesh=mesh, in_specs=in_specs, out_specs=out_specs, check_vma=False)
```

time: 72.1 us -> 54.1 us (0.75)
  local copies, waits for them, and re-layouts: 9.94 us -> 0 us
  Pallas kernels: 59.5 us -> 52 us
    unnamed x19 -> x0, local copies, waits for them, and re-layouts: 9.94 us -> none
    pallas_call x1 -> x2, Pallas kernels: 59.5 us -> 52 us  [the longest x1 49.9 us: local(): pl.pallas_call(kernel, out_shape=shapes, in_specs=[hbm] * 6 + [smem] * 2,...]
where the time goes in v2:
time: 54.1 us; the launch traced here: 54 us
  Pallas kernels  52 us (96%)
  between operations  1.93 us (4%)
    pallas_call x1, Pallas kernels, local(): pl.pallas_call(kernel, out_shape=shapes, in_specs=[hbm] * 6 + [smem] * 2,...  49.9 us
    pallas_call x1, Pallas kernels, local(): pl.pallas_call(finish, out_shape=shapes, in_specs=[hbm] * 7, out_specs=(h...  2.11 us

profile of v2, /device:TPU:1, one launch (start us, length us, event | category | flops | bytes accessed | tf_op | source)
XLA Modules:
  0.0 54.0 jit_solution(11277190525027116495)
XLA Ops:
  1.9 49.9 %grouped_attention_backward.1 = (bf16[256,1280]{1,0:T(8,128)(2,1)}, bf16[256,256]{1,0:T(8,128)(2,1)}, bf16[256,256]{1,0:T(8,128)(2,1)}, bf16[32,256]{1,0:T(8,128...) custom-call(bf16[64,5120]{1,0:T(8,128)(2,1)} %bitcast.12, bf16[64,1024]{1,0:T(8,128)(2,1)} %bitcast.14, ...), custom_call_target="tpu_custom_call" | custom-call | tf_op jit(solution)/shard_map/grouped_attention_backward/pallas_call | solution.py:426
  51.9 2.1 %finish.1 = (bf16[256,1280]{1,0:T(8,128)(2,1)}, bf16[256,256]{1,0:T(8,128)(2,1)}, bf16[256,256]{1,0:T(8,128)(2,1)}, bf16[32,256]{1,0:T(8,128)(2,1)}, bf16[32,256...) custom-call(bf16[256,1280]{1,0:T(8,128)(2,1)} %get-tuple-element.21.refs_0_, ...), custom_call_target="tpu_custom_call" | custom-call | tf_op jit(solution)/shard_map/finish/pallas_call | solution.py:458

commit v3 on v2

v3 whole, which is shorter than its diff:
```python
import math

import jax
import jax.numpy as jnp
from jax import lax
from jax.experimental import pallas as pl
from jax.experimental.pallas import tpu as pltpu
from jax.sharding import PartitionSpec as P

H = 40
KEY_VALUE_HEADS = 8
D = 128
RATIO = H // KEY_VALUE_HEADS
NX = 4
NY = 4
NZ = 4
KV = KEY_VALUE_HEADS // NX
TOK = 64
RESP = NX * TOK
QC = RATIO * D
PRE = 1024
KEYS = PRE + RESP
PIECE = PRE // (2 * NY * NZ)
YROWS = NZ * PIECE
HALF = NY * YROWS
QT = RATIO * RESP
SCALE = D ** -0.5
C2 = SCALE * math.log2(math.e)
MESH = pl.DeviceIdType.MESH
F32 = jnp.float32
BF16 = jnp.bfloat16


def nt(a, b):
    return lax.dot_general(a, b, (((1,), (1,)), ((), ())), preferred_element_type=F32)


def nn(a, b):
    return lax.dot_general(a, b, (((1,), (0,)), ((), ())), preferred_element_type=F32)


def fold(a, op):
    return op(a.reshape(a.shape[0] // 8, 8, a.shape[1]), axis=0)


def kernel(
    q_in, ks_in, vs_in, do_in, pk_in, pv_in, adv_ref, len_ref,
    dq_out, dks_out, dvs_out, dpk_out, dpv_out, qb_out, kvb_out,
    q_st, do_st, c_st, kv_all, k_t, s_buf, dp_buf, p_a, ds_a, p_b, ds_b, acc_kv,
    rs_snd, rs_sib, rs_snd2, rs_y, b_y, b_z,
    xs, xr, kvs, kvr, gl, gzs, gzr, gys, gyr, gss, gsr,
    r0s, r0r, r1s, r1r, bs1, br1, bs2, br2, spare,
):
    g = lax.axis_index("group")
    x = lax.axis_index("tensor")
    dp = lax.axis_index("dp")
    core = lax.rem(g, 2)
    zh = lax.rem(g // 2, NZ)
    y = g // (2 * NZ)
    sib = {"group": g + 1 - 2 * core}

    def xdev(d):
        return {"tensor": lax.rem(x + d, NX)}

    def ydev(d):
        return {"group": lax.rem(y + d, NY) * (2 * NZ) + zh * 2 + core}

    def zdev(d):
        return {"group": y * (2 * NZ) + lax.rem(zh + d, NZ) * 2 + core}

    ypos = y * 2 + core
    zpos = zh * 2 + dp

    def yydev(d):
        p = lax.rem(ypos + d, 2 * NY)
        return {"group": (p // 2) * (2 * NZ) + zh * 2 + lax.rem(p, 2)}

    def zzdev(d):
        p = lax.rem(zpos + d, 2 * NZ)
        return {"group": y * (2 * NZ) + (p // 2) * 2 + core, "dp": lax.rem(p, 2)}

    def remote(src, dst, ss, rs, dev):
        return pltpu.make_async_remote_copy(
            src_ref=src, dst_ref=dst, send_sem=ss, recv_sem=rs, device_id=dev, device_id_type=MESH
        )

    def await_recv(ref, sem):
        remote(ref, ref, spare, sem, sib).wait_recv()

    def await_send(ref, sem):
        remote(ref, ref, sem, spare, sib).wait_send()

    barrier = pltpu.get_barrier_semaphore()
    peers = [xdev(d) for d in range(1, NX)] + [yydev(d) for d in range(1, 2 * NY)]
    peers += [zzdev(d) for d in range(1, 2 * NZ)]
    for dev in peers:
        pl.semaphore_signal(barrier, inc=1, device_id=dev, device_id_type=MESH)

    def xsrc(kind, owner, r):
        return (q_in, do_in)[kind].at[:, pl.ds(pl.multiple_of((owner * KV * RATIO + r) * D, D), D)]

    def xdst(kind, source, r):
        return (q_st, do_st)[kind].at[pl.ds(pl.multiple_of(r * RESP + source * TOK, TOK), TOK)]

    def ksrc(kind, owner, kv):
        return (ks_in, vs_in)[kind].at[:, pl.ds(pl.multiple_of((owner * KV + kv) * D, D), D)]

    def kdst(kind, source, kv):
        return kv_all.at[kv, pl.ds(pl.multiple_of(PRE + source * TOK, TOK), TOK), kind * D : (kind + 1) * D]

    def start_head(r):
        for kind in (0, 1):
            for d in (2, 1, 3):
                src = xsrc(kind, lax.rem(x + d, NX), r)
                remote(src, xdst(kind, x, r), xs.at[kind], xr.at[kind, r], xdev(d)).start()

    def start_keys(kv):
        for kind in (0, 1):
            for d in (2, 1, 3):
                src = ksrc(kind, lax.rem(x + d, NX), kv)
                remote(src, kdst(kind, x, kv), kvs, kvr.at[kv], xdev(d)).start()

    def prow(c, zz, yy, n=PIECE):
        return pl.ds(pl.multiple_of(c * HALF + zz * YROWS + yy * PIECE, PIECE), n)

    def from_z(e):
        return lax.rem(zh + NZ - e, NZ)

    def gather_z(kv):
        own = kv_all.at[kv, prow(core, zh, y)]
        for d in (2, 1, 3):
            remote(own, own, gzs.at[kv], gzr.at[kv, d - 1], zdev(d)).start()

    def gather_y(kv, e):
        blk = kv_all.at[kv, prow(core, from_z(e), y)]
        if e > 0:
            await_recv(blk, gzr.at[kv, e - 1])
        for d in (2, 1, 3):
            remote(blk, blk, gys.at[kv], gyr.at[kv, e], ydev(d)).start()

    def gather_sib(kv, e):
        await_recv(kv_all.at[kv, 0 : (NY - 1) * PIECE], gyr.at[kv, e])
        blk = kv_all.at[kv, prow(core, from_z(e), 0, YROWS)]
        remote(blk, blk, gss.at[kv], gsr.at[kv], sib).start()

    def gather_done(kv):
        await_recv(kv_all.at[kv, 0:HALF], gsr.at[kv])

    for kv in range(KV):
        for kind in (0, 1):
            dst = kv_all.at[kv, prow(core, zh, y), kind * D : (kind + 1) * D]
            pltpu.make_async_copy((pk_in, pv_in)[kind].at[:, kv * D : (kv + 1) * D], dst, gl.at[kv]).start()
    for kv in range(KV):
        await_recv(kv_all.at[kv, 0:PIECE], gl.at[kv])

    pl.semaphore_wait(barrier, len(peers))

    gather_z(0)
    gather_y(0, 0)
    start_head(0)
    start_keys(0)
    gather_z(1)
    gather_y(1, 0)
    for h in range(1, RATIO):
        start_head(h)
    for r in range(KV * RATIO):
        for kind in (0, 1):
            pltpu.make_async_copy(xsrc(kind, x, r), xdst(kind, x, r), xr.at[kind, r]).start()
    for kv in range(KV):
        for kind in (0, 1):
            pltpu.make_async_copy(ksrc(kind, x, kv), kdst(kind, x, kv), kvr.at[kv]).start()
    order = (1, 3, 2)
    for e in order:
        gather_y(0, e)
    start_keys(1)
    start_head(RATIO)
    for e in order:
        gather_y(1, e)
    start_head(RATIO + 1)
    for e in (0,) + order:
        gather_sib(0, e)
    for h in range(2, RATIO):
        start_head(RATIO + h)
    acc_kv[...] = jnp.zeros_like(acc_kv)

    length = len_ref[0, 0]
    tok = lax.broadcasted_iota(jnp.int32, (RESP, 1), 0)
    weight = jnp.full((RESP, 1), adv_ref[0, 0], F32) / jnp.full((RESP, 1), length.astype(F32), F32)
    factor = jnp.where(tok < length, weight, 0.0)

    def seen():
        s = lax.broadcasted_iota(jnp.int32, (RESP, RESP), 0)
        t = lax.broadcasted_iota(jnp.int32, (RESP, RESP), 1)
        return (s <= t) & (s < length)

    nblk = KEYS // RESP

    def blk(b):
        return slice(b * RESP, (b + 1) * RESP)

    def qrows(r):
        return pl.ds(pl.multiple_of(r * RESP, RESP), RESP)

    def arrive(r):
        for kind in (0, 1):
            await_recv((q_st, do_st)[kind].at[qrows(r)], xr.at[kind, r])

    def query_grad(o, ds_old):
        dqh = (nn(k_t[o // RATIO], ds_old[...]) * SCALE).T
        dq_out[:, pl.ds(pl.multiple_of(o * D, D), D)] = dqh.astype(BF16)
        b_y[ypos, pl.ds(o, 1)] = jnp.sum(dqh, axis=0, keepdims=True)

    def step(r, p_new, ds_new, p_old, ds_old):
        arrive(r)
        kv = r // RATIO
        qh = q_st[qrows(r)]
        ch = (do_st[qrows(r)].astype(F32) * factor).astype(BF16)
        c_st[qrows(r)] = ch
        o = r - 1
        top = total = accum = None
        if p_old is not None:
            okv = o // RATIO
            qo = q_st[qrows(o)]
            co = c_st[qrows(o)]

        for b in range(nblk):
            s = nt(kv_all[kv, blk(b), :D], qh)
            if b == nblk - 1:
                s = jnp.where(seen(), s, -1e30)
            s_buf[blk(b)] = s
            m = fold(s, jnp.max)
            top = m if top is None else jnp.maximum(top, m)
        top = jnp.max(top, axis=0, keepdims=True) * C2
        if p_old is not None:
            query_grad(o, ds_old)
        for b in range(nblk):
            if p_old is not None:
                acc_kv[okv, blk(b), D:] += nn(p_old[blk(b)], co)
            dpr = nt(kv_all[kv, blk(b), D:], ch)
            e = jnp.exp2(s_buf[blk(b)] * C2 - top)
            s_buf[blk(b)] = e
            dp_buf[blk(b)] = dpr
            t1 = fold(e, jnp.sum)
            t2 = fold(e * dpr, jnp.sum)
            total = t1 if total is None else total + t1
            accum = t2 if accum is None else accum + t2
        total = jnp.sum(total, axis=0, keepdims=True)
        accum = jnp.sum(accum, axis=0, keepdims=True)
        inv = 1.0 / total
        delta = accum * inv
        for b in range(nblk):
            if p_old is not None:
                acc_kv[okv, blk(b), :D] += nn(ds_old[blk(b)], qo)
            p = s_buf[blk(b)] * inv
            p_new[blk(b)] = p.astype(BF16)
            ds_new[blk(b)] = (p * (dp_buf[blk(b)] - delta)).astype(BF16)

    def rsib(kv):
        return remote(rs_snd.at[kv], rs_sib.at[kv], r0s.at[kv], r0r.at[kv], sib)

    def hops(e, d):
        return 2 * min(e, NZ - e) + min(d, NY - d)

    owners = [(e, d) for e in range(NZ) for d in range(NY) if (e, d) != (0, 0)]
    owners.sort(key=lambda p: -hops(*p))

    def odev(e, d):
        return {"group": lax.rem(y + d, NY) * (2 * NZ) + lax.rem(zh + e, NZ) * 2 + core}

    def zyrows(e, d):
        zz, yy = lax.rem(zh + e, NZ), lax.rem(y + d, NY)
        return pl.ds(pl.multiple_of(zz * YROWS + yy * PIECE, PIECE), PIECE)

    lane = lax.broadcasted_iota(jnp.int32, (1, 2 * D), 1)
    scales = jnp.where(lane < D, SCALE, 1.0)

    def half(kv, c, rows=None):
        base = pl.multiple_of(c * HALF, HALF)
        rows = pl.ds(base, HALF) if rows is None else pl.ds(base + rows.start, rows.size)
        return acc_kv[kv, rows] * scales

    def own_rows(kv, rows):
        return half(kv, core, rows) + rs_sib[kv, rows].astype(F32)

    def reduce_send(kv):
        rsib(kv).wait_recv()
        rs_snd2[kv] = (half(kv, core) + rs_sib[kv].astype(F32)).astype(BF16)
        for i, (e, d) in enumerate(owners):
            remote(rs_snd2.at[kv, zyrows(e, d)], rs_y.at[kv, i], r1s.at[kv], r1r.at[kv], odev(e, d)).start()

    def reduce_done(kv):
        await_recv(rs_y.at[kv], r1r.at[kv])
        acc = own_rows(kv, zyrows(0, 0))
        for i in range(len(owners)):
            acc = acc + rs_y[kv, i].astype(F32)
        dpk_out[:, kv * D : (kv + 1) * D] = acc[:, :D].astype(BF16)
        dpv_out[:, kv * D : (kv + 1) * D] = acc[:, D:].astype(BF16)

    nb = KV * RATIO

    def send_half(kv):
        rs_snd[kv] = half(kv, 1 - core).astype(BF16)
        rsib(kv).start()

    def suffix(kv):
        lanes = slice(kv * D, (kv + 1) * D)
        dks = acc_kv[kv, PRE:, :D] * SCALE
        dvs = acc_kv[kv, PRE:, D:]
        dks_out[:, lanes] = dks.astype(BF16)
        dvs_out[:, lanes] = dvs.astype(BF16)
        b_y[ypos, nb + kv : nb + kv + 1] = jnp.sum(dks, axis=0, keepdims=True)
        b_y[ypos, nb + KV + kv : nb + KV + kv + 1] = jnp.sum(dvs, axis=0, keepdims=True)

    b_y[ypos] = jnp.zeros((16, D), F32)

    def ready(kv):
        gather_done(kv)
        await_recv(kv_all.at[kv, PRE:KEYS], kvr.at[kv])
        k_t[kv] = kv_all[kv, :, :D].T

    bufs_a, bufs_b = (p_a, ds_a), (p_b, ds_b)
    ready(0)
    step(0, *bufs_a, None, None)

    def pair(i, carry):
        @pl.when(i == 0)
        def _():
            for e in (0,) + order:
                gather_sib(1, e)

        @pl.when(i == 2)
        def _():
            ready(1)

        @pl.when(i == 3)
        def _():
            reduce_send(0)

        step(2 * i + 1, *bufs_b, *bufs_a)

        @pl.when(i == 2)
        def _():
            send_half(0)
            suffix(0)

        step(2 * i + 2, *bufs_a, *bufs_b)
        return carry

    lax.fori_loop(0, nb // 2 - 1, pair, 0)
    step(nb - 1, *bufs_b, *bufs_a)

    o = nb - 1
    qo = q_st[o * RESP : (o + 1) * RESP]
    co = c_st[o * RESP : (o + 1) * RESP]
    other = pl.ds(pl.multiple_of((1 - core) * HALF, HALF), HALF)
    mine = pl.ds(pl.multiple_of(core * HALF, HALF), HALF)
    rs_snd[1, :, :D] = ((acc_kv[1, other, :D] + nn(ds_b[other], qo)) * SCALE).astype(BF16)
    rs_snd[1, :, D:] = (acc_kv[1, other, D:] + nn(p_b[other], co)).astype(BF16)
    rsib(1).start()
    for rows in (mine, slice(PRE, KEYS)):
        acc_kv[1, rows, :D] += nn(ds_b[rows], qo)
        acc_kv[1, rows, D:] += nn(p_b[rows], co)
    query_grad(o, ds_b)
    suffix(1)

    for d in range(1, 2 * NY):
        remote(b_y.at[ypos], b_y.at[ypos], bs1, br1, yydev(d)).start()
    reduce_send(1)
    reduce_done(0)
    await_recv(b_y.at[0 : 2 * NY - 1], br1)
    acc = b_y[0]
    for i in range(1, 2 * NY):
        acc = acc + b_y[i]
    b_z[pl.ds(zpos, 1)] = acc[None]
    for d in range(1, 2 * NZ):
        remote(b_z.at[zpos], b_z.at[zpos], bs2, br2, zzdev(d)).start()

    for kind in (0, 1):
        await_send(q_st.at[0 : KV * RATIO * (NX - 1) * TOK], xs.at[kind])
    await_send(q_st.at[0 : 2 * KV * (NX - 1) * TOK], kvs)
    for kv in range(KV):
        await_send(kv_all.at[kv, 0 : (NZ - 1) * PIECE], gzs.at[kv])
        await_send(kv_all.at[kv, 0 : NZ * (NY - 1) * PIECE], gys.at[kv])
        await_send(kv_all.at[kv, 0:HALF], gss.at[kv])
        rsib(kv).wait_send()
    await_send(b_y.at[0 : 2 * NY - 1], bs1)

    await_recv(b_z.at[0 : 2 * NZ - 1], br2)
    acc = b_z[0]
    for i in range(1, 2 * NZ):
        acc = acc + b_z[i]
    qb_out[...] = acc[:nb]
    for kv in range(KV):
        kvb_out[0:1, kv * D : (kv + 1) * D] = acc[nb + kv : nb + kv + 1]
        kvb_out[1:2, kv * D : (kv + 1) * D] = acc[nb + KV + kv : nb + KV + kv + 1]
    reduce_done(1)
    for kv in range(KV):
        await_send(rs_y.at[kv], r1s.at[kv])
    await_send(b_z.at[0 : 2 * NZ - 1], bs2)


def finish(*refs):
    n = (len(refs) - 1) // 2
    sem = refs[-1]
    copies = []
    for i in range(n):
        src, dst = refs[i], refs[n + i]
        parts = 4 if i == 0 else 1
        rows = src.shape[0] // parts
        for j in range(parts):
            part = pl.ds(j * rows, rows)
            copies.append(pltpu.make_async_copy(src.at[part], dst.at[part], sem.at[len(copies)]))
    for copy in copies:
        copy.start()
    for copy in copies:
        copy.wait()


def local(queries, suffix_keys, suffix_values, d_out, prefix_keys, prefix_values, advantages, lengths):
    sds = jax.ShapeDtypeStruct
    dma = pltpu.SemaphoreType.DMA
    hbm = pl.BlockSpec(memory_space=pl.ANY)
    smem = pl.BlockSpec(memory_space=pltpu.SMEM)
    nb = KV * RATIO
    vm = pltpu.VMEM
    shapes = (
        sds((RESP, KV * QC), BF16),
        sds((RESP, KV * D), BF16),
        sds((RESP, KV * D), BF16),
        sds((PIECE, KV * D), BF16),
        sds((PIECE, KV * D), BF16),
        sds((nb, D), F32),
        sds((2, KV * D), F32),
    )
    out = pl.pallas_call(
        kernel,
        out_shape=tuple(vm(s.shape, s.dtype) for s in shapes),
        in_specs=[hbm] * 6 + [smem] * 2,
        out_specs=(pl.BlockSpec(memory_space=vm),) * 7,
        scratch_shapes=[
            vm((KV * QT, D), BF16), vm((KV * QT, D), BF16), vm((KV * QT, D), BF16),
            vm((KV, KEYS, 2 * D), BF16),
            vm((KV, D, KEYS), BF16),
            vm((KEYS, RESP), F32), vm((KEYS, RESP), F32),
            vm((KEYS, RESP), BF16), vm((KEYS, RESP), BF16), vm((KEYS, RESP), BF16), vm((KEYS, RESP), BF16),
            vm((KV, KEYS, 2 * D), F32),
            vm((KV, HALF, 2 * D), BF16), vm((KV, HALF, 2 * D), BF16),
            vm((KV, HALF, 2 * D), BF16), vm((KV, NY * NZ - 1, PIECE, 2 * D), BF16),
            vm((2 * NY, 16, D), F32), vm((2 * NZ, 16, D), F32),
            dma((2,)), dma((2, nb)), dma, dma((KV,)), dma((KV,)),
            dma((KV,)), dma((KV, NZ - 1)), dma((KV,)), dma((KV, NZ)), dma((KV,)), dma((KV,)),
            dma((KV,)), dma((KV,)), dma((KV,)), dma((KV,)),
            dma, dma, dma, dma, dma,
        ],
        compiler_params=pltpu.CompilerParams(
            collective_id=0, has_side_effects=True, vmem_limit_bytes=60 * 1024 * 1024
        ),
        name="grouped_attention_backward",
    )(
        queries[0, 0], suffix_keys[0, 0], suffix_values[0, 0], d_out[0, 0],
        prefix_keys[0], prefix_values[0], advantages, lengths,
    )
    out = pl.pallas_call(
        finish,
        out_shape=shapes,
        in_specs=[hbm] * 7,
        out_specs=(hbm,) * 7,
        scratch_shapes=[dma((10,))],
        compiler_params=pltpu.CompilerParams(vmem_limit_bytes=4 * 1024 * 1024),
        name="finish",
    )(*out)
    dq, dks, dvs, dpk, dpv, qb, kvb = out
    return (dq[None, None], dks[None, None], dvs[None, None], dpk[None], dpv[None], qb.reshape(-1), kvb)


def solution(mesh):
    in_specs = (
        P("dp", "group", "tensor", None),
        P("dp", "group", "tensor", None),
        P("dp", "group", "tensor", None),
        P("dp", "group", "tensor", None),
        P("dp", "group", "tensor"),
        P("dp", "group", "tensor"),
        P("dp", "group"),
        P("dp", "group"),
    )
    out_specs = (
        P("dp", "group", None, "tensor"),
        P("dp", "group", None, "tensor"),
        P("dp", "group", None, "tensor"),
        P("dp", "group", "tensor"),
        P("dp", "group", "tensor"),
        P("tensor"),
        P(None, "tensor"),
    )
    return jax.shard_map(local, mesh=mesh, in_specs=in_specs, out_specs=out_specs, check_vma=False)
```

time: 54.1 us -> 49.2 us (0.909)
  Pallas kernels: 52 us -> 47.1 us
    pallas_call x1, Pallas kernels: 49.9 us -> 46.1 us  [local(): pl.pallas_call(kernel, out_shape=tuple((vm(s.shape, s.dtype) for s in sha...]
    pallas_call x1, Pallas kernels: 2.11 us -> 1.01 us  [local(): pl.pallas_call(finish, out_shape=shapes, in_specs=[hbm] * 7, out_specs=(h...]
where the time goes in v3:
time: 49.2 us; the launch traced here: 49 us
  Pallas kernels  47.1 us (96%)
  between operations  1.93 us (4%)
    pallas_call x1, Pallas kernels, local(): pl.pallas_call(kernel, out_shape=tuple((vm(s.shape, s.dtype) for s in sha...  46.1 us
    pallas_call x1, Pallas kernels, local(): pl.pallas_call(finish, out_shape=shapes, in_specs=[hbm] * 7, out_specs=(h...  1.01 us

profile of v3, /device:TPU:1, one launch (start us, length us, event | category | flops | bytes accessed | tf_op | source)
XLA Modules:
  0.0 49.0 jit_solution(13513904961257241443)
XLA Ops:
  1.9 46.1 %grouped_attention_backward.1 = (bf16[256,1280]{1,0:T(8,128)(2,1)S(1)}, bf16[256,256]{1,0:T(8,128)(2,1)S(1)}, bf16[256,256]{1,0:T(8,128)(2,1)S(1)}, bf16[32,256]...) custom-call(bf16[64,5120]{1,0:T(8,128)(2,1)} %bitcast.12, ...), custom_call_target="tpu_custom_call" | custom-call | tf_op jit(solution)/shard_map/grouped_attention_backward/pallas_call | solution.py:435
  48.0 1.0 %finish.1 = (bf16[256,1280]{1,0:T(8,128)(2,1)}, bf16[256,256]{1,0:T(8,128)(2,1)}, bf16[256,256]{1,0:T(8,128)(2,1)}, bf16[32,256]{1,0:T(8,128)(2,1)}, bf16[32,256...) custom-call(bf16[256,1280]{1,0:T(8,128)(2,1)S(1)} %get-tuple-element.21.refs_0_, ...), custom_call_target="tpu_custom_call" | custom-call | tf_op jit(solution)/shard_map/finish/pallas_call | solution.py:463

commit v4 on v3

--- a/solution.py
+++ b/solution.py
@@ -208,7 +208,7 @@
     def query_grad(o, ds_old):
         dqh = (nn(k_t[o // RATIO], ds_old[...]) * SCALE).T
         dq_out[:, pl.ds(pl.multiple_of(o * D, D), D)] = dqh.astype(BF16)
-        b_y[ypos, pl.ds(o, 1)] = jnp.sum(dqh, axis=0, keepdims=True)
+        b_z[zpos, pl.ds(o, 1)] = jnp.sum(dqh, axis=0, keepdims=True)
 
     def step(r, p_new, ds_new, p_old, ds_old):
         arrive(r)
@@ -255,14 +255,20 @@
             p_new[blk(b)] = p.astype(BF16)
             ds_new[blk(b)] = (p * (dp_buf[blk(b)] - delta)).astype(BF16)
 
-    def rsib(kv):
-        return remote(rs_snd.at[kv], rs_sib.at[kv], r0s.at[kv], r0r.at[kv], sib)
-
-    def hops(e, d):
-        return 2 * min(e, NZ - e) + min(d, NY - d)
-
-    owners = [(e, d) for e in range(NZ) for d in range(NY) if (e, d) != (0, 0)]
-    owners.sort(key=lambda p: -hops(*p))
+    far = (2, 1, 3, 0)
+
+    def zrows(e):
+        return pl.ds(pl.multiple_of(lax.rem(zh + e, NZ) * YROWS, YROWS), YROWS)
+
+    def rsib(kv, e):
+        rows = zrows(e)
+        return remote(rs_snd.at[kv, rows], rs_sib.at[kv, rows], r0s.at[kv], r0r.at[kv, e], sib)
+
+    def send_sib(kv):
+        for e in far:
+            rsib(kv, e).start()
+
+    owners = [(e, d) for e in far for d in far if (e, d) != (0, 0)]
 
     def odev(e, d):
         return {"group": lax.rem(y + d, NY) * (2 * NZ) + lax.rem(zh + e, NZ) * 2 + core}
@@ -283,10 +289,13 @@
         return half(kv, core, rows) + rs_sib[kv, rows].astype(F32)
 
     def reduce_send(kv):
-        rsib(kv).wait_recv()
-        rs_snd2[kv] = (half(kv, core) + rs_sib[kv].astype(F32)).astype(BF16)
-        for i, (e, d) in enumerate(owners):
-            remote(rs_snd2.at[kv, zyrows(e, d)], rs_y.at[kv, i], r1s.at[kv], r1r.at[kv], odev(e, d)).start()
+        for e in far:
+            rsib(kv, e).wait_recv()
+            rs_snd2[kv, zrows(e)] = own_rows(kv, zrows(e)).astype(BF16)
+            for i, (ee, d) in enumerate(owners):
+                if ee == e:
+                    src = rs_snd2.at[kv, zyrows(e, d)]
+                    remote(src, rs_y.at[kv, i], r1s.at[kv], r1r.at[kv], odev(e, d)).start()
 
     def reduce_done(kv):
         await_recv(rs_y.at[kv], r1r.at[kv])
@@ -300,7 +309,7 @@
 
     def send_half(kv):
         rs_snd[kv] = half(kv, 1 - core).astype(BF16)
-        rsib(kv).start()
+        send_sib(kv)
 
     def suffix(kv):
         lanes = slice(kv * D, (kv + 1) * D)
@@ -308,10 +317,10 @@
         dvs = acc_kv[kv, PRE:, D:]
         dks_out[:, lanes] = dks.astype(BF16)
         dvs_out[:, lanes] = dvs.astype(BF16)
-        b_y[ypos, nb + kv : nb + kv + 1] = jnp.sum(dks, axis=0, keepdims=True)
-        b_y[ypos, nb + KV + kv : nb + KV + kv + 1] = jnp.sum(dvs, axis=0, keepdims=True)
-
-    b_y[ypos] = jnp.zeros((16, D), F32)
+        b_z[zpos, nb + kv : nb + kv + 1] = jnp.sum(dks, axis=0, keepdims=True)
+        b_z[zpos, nb + KV + kv : nb + KV + kv + 1] = jnp.sum(dvs, axis=0, keepdims=True)
+
+    b_z[zpos] = jnp.zeros((16, D), F32)
 
     def ready(kv):
         gather_done(kv)
@@ -356,24 +365,24 @@
     mine = pl.ds(pl.multiple_of(core * HALF, HALF), HALF)
     rs_snd[1, :, :D] = ((acc_kv[1, other, :D] + nn(ds_b[other], qo)) * SCALE).astype(BF16)
     rs_snd[1, :, D:] = (acc_kv[1, other, D:] + nn(p_b[other], co)).astype(BF16)
-    rsib(1).start()
+    send_sib(1)
     for rows in (mine, slice(PRE, KEYS)):
         acc_kv[1, rows, :D] += nn(ds_b[rows], qo)
         acc_kv[1, rows, D:] += nn(p_b[rows], co)
     query_grad(o, ds_b)
     suffix(1)
 
+    for d in (4, 3, 5, 2, 6, 1, 7):
+        remote(b_z.at[zpos], b_z.at[zpos], bs2, br2, zzdev(d)).start()
+    reduce_send(1)
+    reduce_done(0)
+    await_recv(b_z.at[0 : 2 * NZ - 1], br2)
+    acc = b_z[0]
+    for i in range(1, 2 * NZ):
+        acc = acc + b_z[i]
+    b_y[pl.ds(ypos, 1)] = acc[None]
     for d in range(1, 2 * NY):
         remote(b_y.at[ypos], b_y.at[ypos], bs1, br1, yydev(d)).start()
-    reduce_send(1)
-    reduce_done(0)
-    await_recv(b_y.at[0 : 2 * NY - 1], br1)
-    acc = b_y[0]
-    for i in range(1, 2 * NY):
-        acc = acc + b_y[i]
-    b_z[pl.ds(zpos, 1)] = acc[None]
-    for d in range(1, 2 * NZ):
-        remote(b_z.at[zpos], b_z.at[zpos], bs2, br2, zzdev(d)).start()
 
     for kind in (0, 1):
         await_send(q_st.at[0 : KV * RATIO * (NX - 1) * TOK], xs.at[kind])
@@ -382,21 +391,21 @@
         await_send(kv_all.at[kv, 0 : (NZ - 1) * PIECE], gzs.at[kv])
         await_send(kv_all.at[kv, 0 : NZ * (NY - 1) * PIECE], gys.at[kv])
         await_send(kv_all.at[kv, 0:HALF], gss.at[kv])
-        rsib(kv).wait_send()
-    await_send(b_y.at[0 : 2 * NY - 1], bs1)
-
-    await_recv(b_z.at[0 : 2 * NZ - 1], br2)
-    acc = b_z[0]
-    for i in range(1, 2 * NZ):
-        acc = acc + b_z[i]
+        await_send(rs_snd.at[kv], r0s.at[kv])
+
+    reduce_done(1)
+    await_recv(b_y.at[0 : 2 * NY - 1], br1)
+    acc = b_y[0]
+    for i in range(1, 2 * NY):
+        acc = acc + b_y[i]
     qb_out[...] = acc[:nb]
     for kv in range(KV):
         kvb_out[0:1, kv * D : (kv + 1) * D] = acc[nb + kv : nb + kv + 1]
         kvb_out[1:2, kv * D : (kv + 1) * D] = acc[nb + KV + kv : nb + KV + kv + 1]
-    reduce_done(1)
     for kv in range(KV):
         await_send(rs_y.at[kv], r1s.at[kv])
     await_send(b_z.at[0 : 2 * NZ - 1], bs2)
+    await_send(b_y.at[0 : 2 * NY - 1], bs1)
 
 
 def finish(*refs):
@@ -449,7 +458,7 @@
             vm((2 * NY, 16, D), F32), vm((2 * NZ, 16, D), F32),
             dma((2,)), dma((2, nb)), dma, dma((KV,)), dma((KV,)),
             dma((KV,)), dma((KV, NZ - 1)), dma((KV,)), dma((KV, NZ)), dma((KV,)), dma((KV,)),
-            dma((KV,)), dma((KV,)), dma((KV,)), dma((KV,)),
+            dma((KV,)), dma((KV, NZ)), dma((KV,)), dma((KV,)),
             dma, dma, dma, dma, dma,
         ],
         compiler_params=pltpu.CompilerParams(

time: 49.2 us -> 47.9 us (0.974)
  Pallas kernels: 47.1 us -> 45.8 us
    pallas_call x1, Pallas kernels: 46.1 us -> 44.8 us  [local(): pl.pallas_call(kernel, out_shape=tuple((vm(s.shape, s.dtype) for s in sha...]
where the time goes in v4:
time: 47.9 us; the launch traced here: 47.8 us
  Pallas kernels  45.8 us (96%)
  between operations  1.93 us (4%)
    pallas_call x1, Pallas kernels, local(): pl.pallas_call(kernel, out_shape=tuple((vm(s.shape, s.dtype) for s in sha...  44.8 us
    pallas_call x1, Pallas kernels, local(): pl.pallas_call(finish, out_shape=shapes, in_specs=[hbm] * 7, out_specs=(h...  1.01 us

profile of v4, /device:TPU:1, one launch (start us, length us, event | category | flops | bytes accessed | tf_op | source)
XLA Modules:
  0.0 47.8 jit_solution(9113273455913943850)
XLA Ops:
  1.9 44.8 %grouped_attention_backward.1 = (bf16[256,1280]{1,0:T(8,128)(2,1)S(1)}, bf16[256,256]{1,0:T(8,128)(2,1)S(1)}, bf16[256,256]{1,0:T(8,128)(2,1)S(1)}, bf16[32,256]...) custom-call(bf16[64,5120]{1,0:T(8,128)(2,1)} %bitcast.12, ...), custom_call_target="tpu_custom_call" | custom-call | tf_op jit(solution)/shard_map/grouped_attention_backward/pallas_call | solution.py:444
  46.8 1.0 %finish.1 = (bf16[256,1280]{1,0:T(8,128)(2,1)}, bf16[256,256]{1,0:T(8,128)(2,1)}, bf16[256,256]{1,0:T(8,128)(2,1)}, bf16[32,256]{1,0:T(8,128)(2,1)}, bf16[32,256...) custom-call(bf16[256,1280]{1,0:T(8,128)(2,1)S(1)} %get-tuple-element.21.refs_0_, ...), custom_call_target="tpu_custom_call" | custom-call | tf_op jit(solution)/shard_map/finish/pallas_call | solution.py:472

commit v5 on v4

--- a/solution.py
+++ b/solution.py
@@ -91,8 +91,8 @@
         remote(ref, ref, sem, spare, sib).wait_send()
 
     barrier = pltpu.get_barrier_semaphore()
-    peers = [xdev(d) for d in range(1, NX)] + [yydev(d) for d in range(1, 2 * NY)]
-    peers += [zzdev(d) for d in range(1, 2 * NZ)]
+    peers = [zzdev(d) for d in (4, 3, 5, 2, 6, 1, 7)]
+    peers += [yydev(d) for d in range(1, 2 * NY)] + [xdev(d) for d in (2, 1, 3)]
     for dev in peers:
         pl.semaphore_signal(barrier, inc=1, device_id=dev, device_id_type=MESH)
 
@@ -224,20 +224,20 @@
             co = c_st[qrows(o)]
 
         for b in range(nblk):
-            s = nt(kv_all[kv, blk(b), :D], qh)
+            s = nt(kv_all[kv, blk(b), :D], qh) * C2
             if b == nblk - 1:
                 s = jnp.where(seen(), s, -1e30)
             s_buf[blk(b)] = s
             m = fold(s, jnp.max)
             top = m if top is None else jnp.maximum(top, m)
-        top = jnp.max(top, axis=0, keepdims=True) * C2
+        top = jnp.max(top, axis=0, keepdims=True)
         if p_old is not None:
             query_grad(o, ds_old)
         for b in range(nblk):
             if p_old is not None:
                 acc_kv[okv, blk(b), D:] += nn(p_old[blk(b)], co)
             dpr = nt(kv_all[kv, blk(b), D:], ch)
-            e = jnp.exp2(s_buf[blk(b)] * C2 - top)
+            e = jnp.exp2(s_buf[blk(b)] - top)
             s_buf[blk(b)] = e
             dp_buf[blk(b)] = dpr
             t1 = fold(e, jnp.sum)
@@ -322,10 +322,16 @@
 
     b_z[zpos] = jnp.zeros((16, D), F32)
 
+    def turn(kv, c):
+        rows = pl.ds(pl.multiple_of(c * HALF, HALF), HALF)
+        k_t[kv, :, rows] = kv_all[kv, rows, :D].T
+
     def ready(kv):
+        turn(kv, core)
+        await_recv(kv_all.at[kv, PRE:KEYS], kvr.at[kv])
+        k_t[kv, :, PRE:] = kv_all[kv, PRE:, :D].T
         gather_done(kv)
-        await_recv(kv_all.at[kv, PRE:KEYS], kvr.at[kv])
-        k_t[kv] = kv_all[kv, :, :D].T
+        turn(kv, 1 - core)
 
     bufs_a, bufs_b = (p_a, ds_a), (p_b, ds_b)
     ready(0)
@@ -366,14 +372,15 @@
     rs_snd[1, :, :D] = ((acc_kv[1, other, :D] + nn(ds_b[other], qo)) * SCALE).astype(BF16)
     rs_snd[1, :, D:] = (acc_kv[1, other, D:] + nn(p_b[other], co)).astype(BF16)
     send_sib(1)
-    for rows in (mine, slice(PRE, KEYS)):
-        acc_kv[1, rows, :D] += nn(ds_b[rows], qo)
-        acc_kv[1, rows, D:] += nn(p_b[rows], co)
     query_grad(o, ds_b)
+    acc_kv[1, PRE:, :D] += nn(ds_b[PRE:], qo)
+    acc_kv[1, PRE:, D:] += nn(p_b[PRE:], co)
     suffix(1)
 
     for d in (4, 3, 5, 2, 6, 1, 7):
         remote(b_z.at[zpos], b_z.at[zpos], bs2, br2, zzdev(d)).start()
+    acc_kv[1, mine, :D] += nn(ds_b[mine], qo)
+    acc_kv[1, mine, D:] += nn(p_b[mine], co)
     reduce_send(1)
     reduce_done(0)
     await_recv(b_z.at[0 : 2 * NZ - 1], br2)

time: 47.9 us -> 48.1 us (level)
  no operation moved by 1% of the time
where the time goes in v5:
time: 48.1 us; the launch traced here: 47.9 us
  Pallas kernels  46 us (96%)
  between operations  1.93 us (4%)
    pallas_call x1, Pallas kernels, local(): pl.pallas_call(kernel, out_shape=tuple((vm(s.shape, s.dtype) for s in sha...  45 us
    pallas_call x1, Pallas kernels, local(): pl.pallas_call(finish, out_shape=shapes, in_specs=[hbm] * 7, out_specs=(h...  1.01 us

profile of v5, /device:TPU:1, one launch (start us, length us, event | category | flops | bytes accessed | tf_op | source)
XLA Modules:
  0.0 47.9 jit_solution(9273063087843222401)
XLA Ops:
  1.9 45.0 %grouped_attention_backward.1 = (bf16[256,1280]{1,0:T(8,128)(2,1)S(1)}, bf16[256,256]{1,0:T(8,128)(2,1)S(1)}, bf16[256,256]{1,0:T(8,128)(2,1)S(1)}, bf16[32,256]...) custom-call(bf16[64,5120]{1,0:T(8,128)(2,1)} %bitcast.12, ...), custom_call_target="tpu_custom_call" | custom-call | tf_op jit(solution)/shard_map/grouped_attention_backward/pallas_call | solution.py:451
  46.9 1.0 %finish.1 = (bf16[256,1280]{1,0:T(8,128)(2,1)}, bf16[256,256]{1,0:T(8,128)(2,1)}, bf16[256,256]{1,0:T(8,128)(2,1)}, bf16[32,256]{1,0:T(8,128)(2,1)}, bf16[32,256...) custom-call(bf16[256,1280]{1,0:T(8,128)(2,1)S(1)} %get-tuple-element.21.refs_0_, ...), custom_call_target="tpu_custom_call" | custom-call | tf_op jit(solution)/shard_map/finish/pallas_call | solution.py:479

commit v6 on v4

--- a/solution.py
+++ b/solution.py
@@ -289,13 +289,16 @@
         return half(kv, core, rows) + rs_sib[kv, rows].astype(F32)
 
     def reduce_send(kv):
-        for e in far:
-            rsib(kv, e).wait_recv()
-            rs_snd2[kv, zrows(e)] = own_rows(kv, zrows(e)).astype(BF16)
-            for i, (ee, d) in enumerate(owners):
-                if ee == e:
-                    src = rs_snd2.at[kv, zyrows(e, d)]
-                    remote(src, rs_y.at[kv, i], r1s.at[kv], r1r.at[kv], odev(e, d)).start()
+        for group in ((2,), (1, 3, 0)):
+            for e in group:
+                rsib(kv, e).wait_recv()
+                rs_snd2[kv, zrows(e)] = own_rows(kv, zrows(e)).astype(BF16)
+            for d in far:
+                for e in group:
+                    if (e, d) != (0, 0):
+                        src = rs_snd2.at[kv, zyrows(e, d)]
+                        i = owners.index((e, d))
+                        remote(src, rs_y.at[kv, i], r1s.at[kv], r1r.at[kv], odev(e, d)).start()
 
     def reduce_done(kv):
         await_recv(rs_y.at[kv], r1r.at[kv])
@@ -381,7 +384,7 @@
     for i in range(1, 2 * NZ):
         acc = acc + b_z[i]
     b_y[pl.ds(ypos, 1)] = acc[None]
-    for d in range(1, 2 * NY):
+    for d in (4, 3, 5, 2, 6, 1, 7):
         remote(b_y.at[ypos], b_y.at[ypos], bs1, br1, yydev(d)).start()
 
     for kind in (0, 1):

time: 47.9 us -> 47.5 us (level)
  no operation moved by 1% of the time
where the time goes in v6:
time: 47.5 us; the launch traced here: 47.4 us
  Pallas kernels  45.4 us (96%)
  between operations  1.93 us (4%)
    pallas_call x1, Pallas kernels, local(): pl.pallas_call(kernel, out_shape=tuple((vm(s.shape, s.dtype) for s in sha...  44.4 us
    pallas_call x1, Pallas kernels, local(): pl.pallas_call(finish, out_shape=shapes, in_specs=[hbm] * 7, out_specs=(h...  1.01 us

profile of v6, /device:TPU:1, one launch (start us, length us, event | category | flops | bytes accessed | tf_op | source)
XLA Modules:
  0.0 47.4 jit_solution(6331400273494446239)
XLA Ops:
  1.9 44.4 %grouped_attention_backward.1 = (bf16[256,1280]{1,0:T(8,128)(2,1)S(1)}, bf16[256,256]{1,0:T(8,128)(2,1)S(1)}, bf16[256,256]{1,0:T(8,128)(2,1)S(1)}, bf16[32,256]...) custom-call(bf16[64,5120]{1,0:T(8,128)(2,1)} %bitcast.12, ...), custom_call_target="tpu_custom_call" | custom-call | tf_op jit(solution)/shard_map/grouped_attention_backward/pallas_call | solution.py:447
  46.4 1.0 %finish.1 = (bf16[256,1280]{1,0:T(8,128)(2,1)}, bf16[256,256]{1,0:T(8,128)(2,1)}, bf16[256,256]{1,0:T(8,128)(2,1)}, bf16[32,256]{1,0:T(8,128)(2,1)}, bf16[32,256...) custom-call(bf16[256,1280]{1,0:T(8,128)(2,1)S(1)} %get-tuple-element.21.refs_0_, ...), custom_call_target="tpu_custom_call" | custom-call | tf_op jit(solution)/shard_map/finish/pallas_call | solution.py:475
